TPU v7x, 256 devices: a whole 4x4x8 slice. The times are simulated.
256 devices in a mesh: tp: 4 (over x), ep: 64 (over z, y, core).
Axes of the slice: x: 4, y: 4, z: 8, core: 2. Of those that a mesh axis runs over, the one named last changes fastest.
Arguments:
- tokens: bfloat16 [32768, 2048], P(('tp', 'ep')), may hold values from -6 to 6
- expert_ids: int32 [32768, 2], P(('tp', 'ep')), may hold values from 0 to 255, all different within a row; in each aligned block of 128 rows (0 to 127, 128 to 255, ...) at most 2 rows name the same one
- gate_weights: float32 [32768, 2], P(('tp', 'ep')), may hold values from 0.1 to 1
- grad_out: bfloat16 [32768, 2048], P(('tp', 'ep')), may hold values from -6 to 6
- expert_gate: bfloat16 [256, 2048, 512], P(('tp', 'ep')), may hold values from -0.125 to 0.125
- expert_up: bfloat16 [256, 2048, 512], P(('tp', 'ep')), may hold values from -0.125 to 0.125
- expert_down: bfloat16 [256, 512, 2048], P(('tp', 'ep')), may hold values from -0.25 to 0.25
- shared_gate: bfloat16 [2048, 512], P(None, 'tp'), may hold values from -0.125 to 0.125
- shared_up: bfloat16 [2048, 512], P(None, 'tp'), may hold values from -0.125 to 0.125
- shared_down: bfloat16 [512, 2048], P('tp'), may hold values from -0.25 to 0.25
- shared_switch: bfloat16 [2048], replicated, may hold values from -0.29882812 to 0.29882812
Outputs:
- mixed: bfloat16 [32768, 2048], P(('tp', 'ep'))
- grad_tokens: bfloat16 [32768, 2048], P(('tp', 'ep'))
- gate_grad: float32 [32768, 2], P(('tp', 'ep'))
Inputs may be any that keep to these rules, and one draw needn't show every extreme that they name: `expert_ids`: each row names 2 different experts; among the rows of one device no expert is named more than 2 times, a bound that some block reaches.
All inputs are finite; a program needn't handle non-finite values.
Results may differ from a plain program's by a relative error of at most 0.019.
Values may be sent and summed in bfloat16 or wider, within the bound.
No kernel may reach another device: no remote copies, remote signals or barrier semaphores. Data moves between devices by JAX's collectives and lax.ppermute only.
A program may use at most 128 MiB of HBM per device.

v0:
```python
import jax
import jax.numpy as jnp
from jax import lax
from jax.sharding import PartitionSpec as P


def silu_grad(argument):
    gate_sig = jax.nn.sigmoid(argument)
    return gate_sig * (1.0 + argument * (1.0 - gate_sig))


def expert_slots(expert_ids, experts, capacity):
    chosen = expert_ids.reshape(-1)
    onehot = (chosen[:, None] == jnp.arange(experts, dtype=jnp.int32)[None, :]).astype(jnp.int32)
    before = jnp.cumsum(onehot, axis=0) - onehot
    position = jnp.sum(before * onehot, axis=1)
    return chosen * capacity + position


def expert_forward(slot_rows, weighting, expert_gate, expert_up, expert_down):
    pre_gate = jnp.einsum(
        "sjcd,jdf->sjcf", slot_rows, expert_gate, preferred_element_type=jnp.float32
    )
    pre_up = jnp.einsum("sjcd,jdf->sjcf", slot_rows, expert_up, preferred_element_type=jnp.float32)
    hidden = (jax.nn.silu(pre_gate) * pre_up).astype(jnp.bfloat16)
    output = jnp.einsum("sjcf,jfd->sjcd", hidden, expert_down, preferred_element_type=jnp.float32)
    routed = (weighting[..., None] * output).astype(jnp.bfloat16)
    return (pre_gate, pre_up, output, routed)


def expert_backward(
    cot_rows, weighting, pre_gate, pre_up, output, expert_gate, expert_up, expert_down
):
    cotangent = cot_rows.astype(jnp.float32)
    slot_grad = jnp.sum(cotangent * output, axis=3)
    scaled = (weighting[..., None] * cotangent).astype(jnp.bfloat16)
    hidden_grad = jnp.einsum(
        "sjcd,jfd->sjcf", scaled, expert_down, preferred_element_type=jnp.float32
    )
    gate_part = (hidden_grad * pre_up * silu_grad(pre_gate)).astype(jnp.bfloat16)
    up_part = (hidden_grad * jax.nn.silu(pre_gate)).astype(jnp.bfloat16)
    input_grad = (
        jnp.einsum("sjcf,jdf->sjcd", gate_part, expert_gate, preferred_element_type=jnp.float32)
        + jnp.einsum("sjcf,jdf->sjcd", up_part, expert_up, preferred_element_type=jnp.float32)
    ).astype(jnp.bfloat16)
    return (input_grad, slot_grad)


def local(
    tokens,
    expert_ids,
    gate_weights,
    grad_out,
    expert_gate,
    expert_up,
    expert_down,
    shared_gate,
    shared_up,
    shared_down,
    shared_switch,
):
    tp_count = lax.axis_size("tp")
    ep_count = lax.axis_size("ep")
    held_experts = expert_gate.shape[0]
    experts = held_experts * tp_count * ep_count
    tok_rows = tokens.shape[0]
    model_width = tokens.shape[1]
    routes_each = expert_ids.shape[1]
    capacity = max(2, 2 * tok_rows * routes_each // experts)
    slot_count = experts * capacity
    layout = (tp_count, ep_count, held_experts * capacity)
    sources = tp_count * ep_count
    slot_shape = (sources, held_experts, capacity, model_width)
    slot_index = expert_slots(expert_ids, experts, capacity)
    send_rows = (
        jnp.zeros((slot_count, model_width), jnp.bfloat16)
        .at[slot_index]
        .set(jnp.repeat(tokens, routes_each, axis=0))
    )
    send_gates = jnp.zeros((slot_count,), jnp.float32).at[slot_index].set(gate_weights.reshape(-1))
    send_cot = (
        jnp.zeros((slot_count, model_width), jnp.bfloat16)
        .at[slot_index]
        .set(jnp.repeat(grad_out, routes_each, axis=0))
    )
    arrived, arrived_gates = (
        lax.all_to_all(
            lax.all_to_all(
                send_rows.reshape(layout + (model_width,)),
                "tp",
                split_axis=0,
                concat_axis=0,
                tiled=True,
            ),
            "ep",
            split_axis=1,
            concat_axis=1,
            tiled=True,
        ),
        lax.all_to_all(
            lax.all_to_all(
                send_gates.reshape(layout).astype(jnp.bfloat16),
                "tp",
                split_axis=0,
                concat_axis=0,
                tiled=True,
            ),
            "ep",
            split_axis=1,
            concat_axis=1,
            tiled=True,
        ).astype(jnp.float32),
    )
    weighting = arrived_gates.reshape(sources, held_experts, capacity)
    pre_gate, pre_up, output, routed = expert_forward(
        arrived.reshape(slot_shape), weighting, expert_gate, expert_up, expert_down
    )
    routed_back = lax.all_to_all(
        lax.all_to_all(
            routed.reshape(layout + (model_width,)), "tp", split_axis=0, concat_axis=0, tiled=True
        ),
        "ep",
        split_axis=1,
        concat_axis=1,
        tiled=True,
    )
    arrived_cot = lax.all_to_all(
        lax.all_to_all(
            send_cot.reshape(layout + (model_width,)), "tp", split_axis=0, concat_axis=0, tiled=True
        ),
        "ep",
        split_axis=1,
        concat_axis=1,
        tiled=True,
    )
    input_grad, slot_grad = expert_backward(
        arrived_cot.reshape(slot_shape),
        weighting,
        pre_gate,
        pre_up,
        output,
        expert_gate,
        expert_up,
        expert_down,
    )
    grad_back, gate_back = (
        lax.all_to_all(
            lax.all_to_all(
                input_grad.reshape(layout + (model_width,)),
                "tp",
                split_axis=0,
                concat_axis=0,
                tiled=True,
            ),
            "ep",
            split_axis=1,
            concat_axis=1,
            tiled=True,
        ),
        lax.all_to_all(
            lax.all_to_all(
                slot_grad.reshape(layout).astype(jnp.bfloat16),
                "tp",
                split_axis=0,
                concat_axis=0,
                tiled=True,
            ),
            "ep",
            split_axis=1,
            concat_axis=1,
            tiled=True,
        ).astype(jnp.float32),
    )
    routed_sum = (
        routed_back.reshape(slot_count, model_width)[slot_index]
        .astype(jnp.float32)
        .reshape(tok_rows, routes_each, model_width)
        .sum(axis=1)
    )
    routed_grad = (
        grad_back.reshape(slot_count, model_width)[slot_index]
        .astype(jnp.float32)
        .reshape(tok_rows, routes_each, model_width)
        .sum(axis=1)
    )
    gate_grad = gate_back.reshape(slot_count)[slot_index].reshape(tok_rows, routes_each)
    switch_logit = jnp.dot(tokens, shared_switch, preferred_element_type=jnp.float32)
    switch = jax.nn.sigmoid(switch_logit)
    shared_cot = (switch[:, None] * grad_out.astype(jnp.float32)).astype(jnp.bfloat16)
    gathered = lax.all_gather(tokens, "tp", axis=0, tiled=True)
    shared_pre_gate = jnp.dot(gathered, shared_gate, preferred_element_type=jnp.float32)
    shared_pre_up = jnp.dot(gathered, shared_up, preferred_element_type=jnp.float32)
    shared_hidden = (jax.nn.silu(shared_pre_gate) * shared_pre_up).astype(jnp.bfloat16)
    shared = lax.psum_scatter(
        jnp.dot(shared_hidden, shared_down, preferred_element_type=jnp.float32).astype(
            jnp.bfloat16
        ),
        "tp",
        scatter_dimension=0,
        tiled=True,
    ).astype(jnp.float32)
    cot_gathered = lax.all_gather(shared_cot, "tp", axis=0, tiled=True)
    shared_hidden_grad = jnp.einsum(
        "td,fd->tf", cot_gathered, shared_down, preferred_element_type=jnp.float32
    )
    shared_gate_part = (shared_hidden_grad * shared_pre_up * silu_grad(shared_pre_gate)).astype(
        jnp.bfloat16
    )
    shared_up_part = (shared_hidden_grad * jax.nn.silu(shared_pre_gate)).astype(jnp.bfloat16)
    shared_input_grad = lax.psum_scatter(
        (
            jnp.einsum(
                "tf,df->td", shared_gate_part, shared_gate, preferred_element_type=jnp.float32
            )
            + jnp.einsum("tf,df->td", shared_up_part, shared_up, preferred_element_type=jnp.float32)
        ).astype(jnp.bfloat16),
        "tp",
        scatter_dimension=0,
        tiled=True,
    ).astype(jnp.float32)
    mixed = (switch[:, None] * shared + routed_sum).astype(jnp.bfloat16)
    switch_grad = switch * (1.0 - switch) * jnp.sum(grad_out.astype(jnp.float32) * shared, axis=1)
    grad_tokens = (
        shared_input_grad
        + routed_grad
        + switch_grad[:, None] * shared_switch.astype(jnp.float32)[None, :]
    ).astype(jnp.bfloat16)
    return (mixed, grad_tokens, gate_grad)


def solution(mesh):
    placed = (
        P(("tp", "ep"), None),
        P(("tp", "ep"), None),
        P(("tp", "ep"), None),
        P(("tp", "ep"), None),
        P(("tp", "ep"), None, None),
        P(("tp", "ep"), None, None),
        P(("tp", "ep"), None, None),
        P(None, "tp"),
        P(None, "tp"),
        P("tp", None),
        P(),
    )
    return jax.shard_map(
        local,
        mesh=mesh,
        in_specs=placed,
        out_specs=(P(("tp", "ep"), None), P(("tp", "ep"), None), P(("tp", "ep"), None)),
        check_vma=False,
    )
```

profile of v0, /device:TPU:1, one launch (start us, length us, event | category | flops | bytes accessed | tf_op | source)
XLA Modules:
  0.0 522.7 jit_solution(11906621634185771568)
XLA Ops:
  12.6 8.7 %all_to_all.60 = bf16[4,64,2]{1,2,0:T(2,128)(2,1)S(1)} all-to-all(bf16[4,64,2]{1,2,0:T(2,128)(2,1)S(1)} %copy.82), channel_id=1, replica_groups=mesh['tp'=4,'ep'=64] {'tp'}, dimensions={0} | all-to-all | bytes 2048 | tf_op jit(solution)/shard_map/all_to_all | solution.py:101
  22.1 13.8 %all-to-all-start.1 = ((bf16[4,64,2]{0,2,1:T(2,128)(2,1)}), bf16[4,64,2]{0,2,1:T(2,128)(2,1)S(1)}, u32[]{:S(2)}, u32[]{:S(2)}) async-start(bf16[4,64,2]{0,2,1:T(2,128)(2,1)} %copy.83), calls=%async_computation.2 | async-start | bytes 65536 | tf_op jit(solution)/shard_map/all_to_all | solution.py:100
  42.7 4.4 reshape.170
  47.1 4.5 all-to-all-start.2
  54.5 4.4 scatter_custom_fusion.2
  58.9 4.4 reshape.179
  63.3 14.3 %all-to-all-done.2 = bf16[4,64,2,2048]{3,2,1,0:T(2,128)(2,1)} async-done(((bf16[4,64,2,2048]{3,2,1,0:T(2,128)(2,1)}), bf16[4,64,2,2048]{3,2,1,0:T(2,128)(2,1)}, u32[]{:S(2)}, u32[]{:S(2)}) %all-to-all-start.2) | async-done | bytes 2097184 | tf_op jit(solution)/shard_map/all_to_all | solution.py:88
  77.6 4.7 all-to-all-start.6
  82.3 5.5 %copy.85 = bf16[4,64,2,2048]{3,2,0,1:T(2,128)(2,1)} copy(bf16[4,64,2,2048]{3,2,1,0:T(2,128)(2,1)} %all-to-all-done.2) | data formatting | bytes 4194304 | tf_op jit(solution)/shard_map/all_to_all | solution.py:88
  87.8 19.7 %all-to-all-done.6 = bf16[4,64,2,2048]{3,2,1,0:T(2,128)(2,1)} async-done(((bf16[4,64,2,2048]{3,2,1,0:T(2,128)(2,1)}), bf16[4,64,2,2048]{3,2,1,0:T(2,128)(2,1)}, u32[]{:S(2)}, u32[]{:S(2)}) %all-to-all-start.6) | async-done | bytes 2097184 | tf_op jit(solution)/shard_map/all_to_all | solution.py:128
  107.4 12.4 %all-to-all-start.3 = ((bf16[4,64,2,2048]{3,2,0,1:T(2,128)(2,1)}), bf16[4,64,2,2048]{3,2,0,1:T(2,128)(2,1)}, u32[]{:S(2)}, u32[]{:S(2)}) async-start(bf16[4,64,2,2048]{3,2,0,1:T(2,128)(2,1)} %copy.85), calls=%async_computation.4 | async-start | bytes 4194304 | tf_op jit(solution)/shard_map/all_to_all | solution.py:87
  119.9 5.4 %copy.90 = bf16[4,64,2,2048]{3,2,0,1:T(2,128)(2,1)} copy(bf16[4,64,2,2048]{3,2,1,0:T(2,128)(2,1)} %all-to-all-done.6) | data formatting | bytes 4194304 | tf_op jit(solution)/shard_map/all_to_all | solution.py:128
  125.2 44.2 %all-to-all-done.3 = bf16[4,64,2,2048]{3,2,0,1:T(2,128)(2,1)} async-done(((bf16[4,64,2,2048]{3,2,0,1:T(2,128)(2,1)}), bf16[4,64,2,2048]{3,2,0,1:T(2,128)(2,1)}, u32[]{:S(2)}, u32[]{:S(2)}) %all-to-all-start.3) | async-done | bytes 2097184 | tf_op jit(solution)/shard_map/all_to_all | solution.py:87
  169.5 7.2 %all-to-all-start.7 = ((bf16[4,64,2,2048]{3,2,0,1:T(2,128)(2,1)}), bf16[4,64,2,2048]{3,2,0,1:T(2,128)(2,1)}, u32[]{:S(2)}, u32[]{:S(2)}) async-start(bf16[4,64,2,2048]{3,2,0,1:T(2,128)(2,1)} %copy.90), calls=%async_computation.9 | async-start | bytes 4194304 | tf_op jit(solution)/shard_map/all_to_all | solution.py:127
  184.3 41.9 %all-to-all-done.7 = bf16[4,64,2,2048]{3,2,0,1:T(2,128)(2,1)} async-done(((bf16[4,64,2,2048]{3,2,0,1:T(2,128)(2,1)}), bf16[4,64,2,2048]{3,2,0,1:T(2,128)(2,1)}, u32[]{:S(2)}, u32[]{:S(2)}) %all-to-all-start.7) | async-done | bytes 2097184 | tf_op jit(solution)/shard_map/all_to_all | solution.py:127
  232.2 4.6 all-to-all-start.4
  243.2 22.4 %all-to-all-done.4 = bf16[4,64,2,2048]{3,1,2,0:T(8,128)(2,1)} async-done(((bf16[4,64,2,2048]{3,1,2,0:T(8,128)(2,1)}), bf16[4,64,2,2048]{3,1,2,0:T(8,128)(2,1)}, u32[]{:S(2)}, u32[]{:S(2)}) %all-to-all-start.4) | async-done | bytes 2097184 | tf_op jit(solution)/shard_map/all_to_all | solution.py:119
  265.6 4.6 copy.88
  270.2 14.0 %all-to-all-start.5 = ((bf16[4,64,2,2048]{3,0,2,1:T(4,128)(2,1)}), bf16[4,64,2,2048]{3,0,2,1:T(4,128)(2,1)}, u32[]{:S(2)}, u32[]{:S(2)}) async-start(bf16[4,64,2,2048]{3,0,2,1:T(4,128)(2,1)} %copy.88), calls=%async_computation.6 | async-start | bytes 4194304 | tf_op jit(solution)/shard_map/all_to_all | solution.py:118
  285.2 48.6 %all-to-all-done.5 = bf16[4,64,2,2048]{3,0,2,1:T(4,128)(2,1)} async-done(((bf16[4,64,2,2048]{3,0,2,1:T(4,128)(2,1)}), bf16[4,64,2,2048]{3,0,2,1:T(4,128)(2,1)}, u32[]{:S(2)}, u32[]{:S(2)}) %all-to-all-start.5) | async-done | bytes 2097184 | tf_op jit(solution)/shard_map/all_to_all | solution.py:118
  337.1 5.1 copy.89
  342.2 4.3 reshape.177
  346.5 4.2 gather_fusion
  369.2 4.5 all-to-all-start.8
  374.4 38.7 %all-to-all-done.8 = bf16[4,64,2,2048]{3,1,2,0:T(8,128)(2,1)} async-done(((bf16[4,64,2,2048]{3,1,2,0:T(8,128)(2,1)}), bf16[4,64,2,2048]{3,1,2,0:T(8,128)(2,1)}, u32[]{:S(2)}, u32[]{:S(2)}) %all-to-all-start.8) | async-done | bytes 2097184 | tf_op jit(solution)/shard_map/all_to_all | solution.py:148
  413.1 10.6 %all-to-all-start.11 = ((bf16[4,64,2]{0,2,1:T(2,128)(2,1)}), bf16[4,64,2]{0,2,1:T(2,128)(2,1)S(1)}, u32[]{:S(2)}, u32[]{:S(2)}) async-start(bf16[4,64,2]{0,2,1:T(2,128)(2,1)} %copy.96), calls=%async_computation.13 | async-start | bytes 65536 | tf_op jit(solution)/shard_map/all_to_all | solution.py:160
  423.8 4.6 copy.93
  433.5 10.6 %all-to-all-start.9 = ((bf16[4,64,2,2048]{3,0,2,1:T(4,128)(2,1)}), bf16[4,64,2,2048]{3,0,2,1:T(4,128)(2,1)}, u32[]{:S(2)}, u32[]{:S(2)}) async-start(bf16[4,64,2,2048]{3,0,2,1:T(4,128)(2,1)} %copy.93), calls=%async_computation.11 | async-start | bytes 4194304 | tf_op jit(solution)/shard_map/all_to_all | solution.py:147
  444.5 4.2 add_convert_fusion.1
  451.9 41.9 %all-to-all-done.9 = bf16[4,64,2,2048]{3,0,2,1:T(4,128)(2,1)} async-done(((bf16[4,64,2,2048]{3,0,2,1:T(4,128)(2,1)}), bf16[4,64,2,2048]{3,0,2,1:T(4,128)(2,1)}, u32[]{:S(2)}, u32[]{:S(2)}) %all-to-all-start.9) | async-done | bytes 2097184 | tf_op jit(solution)/shard_map/all_to_all | solution.py:147
  493.7 5.1 copy.94
  503.0 4.2 gather_fusion.1
  (126 shorter events, 80.1 us)
Async XLA Ops:
  7.2 222.0 %copy-start = (bf16[1,512,2048]{2,1,0:T(8,128)(2,1)S(1)}, bf16[1,512,2048]{2,1,0:T(8,128)(2,1)}, u32[]{:S(2)}) copy-start(bf16[1,512,2048]{2,1,0:T(8,128)(2,1)} %param.17) | copy-start | bytes 6291460
  7.2 28.7 %copy-start.2 = (bf16[128,2048]{1,0:T(8,128)(2,1)S(1)}, bf16[128,2048]{1,0:T(8,128)(2,1)}, u32[]{:S(2)}) copy-start(bf16[128,2048]{1,0:T(8,128)(2,1)} %param.11) | copy-start | bytes 1572868
  22.1 25.0 %all-to-all-start.1 = ((bf16[4,64,2]{0,2,1:T(2,128)(2,1)}), bf16[4,64,2]{0,2,1:T(2,128)(2,1)S(1)}, u32[]{:S(2)}, u32[]{:S(2)}) async-start(bf16[4,64,2]{0,2,1:T(2,128)(2,1)} %copy.83), calls=%async_computation.2 | async-start | bytes 65536 | tf_op jit(solution)/shard_map/all_to_all | solution.py:100
  47.1 30.5 %all-to-all-start.2 = ((bf16[4,64,2,2048]{3,2,1,0:T(2,128)(2,1)}), bf16[4,64,2,2048]{3,2,1,0:T(2,128)(2,1)}, u32[]{:S(2)}, u32[]{:S(2)}) async-start(bf16[4,64,2,2048]{3,2,1,0:T(2,128)(2,1)} %reshape.170), calls=%async_computation.3 | async-start | bytes 4194304 | tf_op jit(solution)/shard_map/all_to_all | solution.py:88
  77.6 29.8 %all-to-all-start.6 = ((bf16[4,64,2,2048]{3,2,1,0:T(2,128)(2,1)}), bf16[4,64,2,2048]{3,2,1,0:T(2,128)(2,1)}, u32[]{:S(2)}, u32[]{:S(2)}) async-start(bf16[4,64,2,2048]{3,2,1,0:T(2,128)(2,1)} %reshape.179), calls=%async_computation.8 | async-start | bytes 4194304 | tf_op jit(solution)/shard_map/all_to_all | solution.py:128
  107.4 62.0 %all-to-all-start.3 = ((bf16[4,64,2,2048]{3,2,0,1:T(2,128)(2,1)}), bf16[4,64,2,2048]{3,2,0,1:T(2,128)(2,1)}, u32[]{:S(2)}, u32[]{:S(2)}) async-start(bf16[4,64,2,2048]{3,2,0,1:T(2,128)(2,1)} %copy.85), calls=%async_computation.4 | async-start | bytes 4194304 | tf_op jit(solution)/shard_map/all_to_all | solution.py:87
  169.5 56.8 %all-to-all-start.7 = ((bf16[4,64,2,2048]{3,2,0,1:T(2,128)(2,1)}), bf16[4,64,2,2048]{3,2,0,1:T(2,128)(2,1)}, u32[]{:S(2)}, u32[]{:S(2)}) async-start(bf16[4,64,2,2048]{3,2,0,1:T(2,128)(2,1)} %copy.90), calls=%async_computation.9 | async-start | bytes 4194304 | tf_op jit(solution)/shard_map/all_to_all | solution.py:127
  176.7 60.6 %all-gather.3.cloned.1.call-start = ((), (), s32[]{:S(2)}) async-start(), calls=%async_computation.14 | async-start | bytes 2621440 | tf_op jit(solution)/shard_map/all_gather | solution.py:190
  177.6 2.9 copy-start.17
  180.5 1.6 copy-start.8
  182.1 47.1 %copy-start.14 = (f32[256,1,2,512]{3,0,2,1:T(8,128)}, f32[256,1,2,512]{3,0,2,1:T(8,128)S(1)}, u32[]{:S(2)}) copy-start(f32[256,1,2,512]{3,0,2,1:T(8,128)S(1)} %fusion.13) | copy-start | bytes 3145732
  226.3 2.9 copy-start.19
  232.2 5.1 copy-start.12
  232.2 33.4 %all-to-all-start.4 = ((bf16[4,64,2,2048]{3,1,2,0:T(8,128)(2,1)}), bf16[4,64,2,2048]{3,1,2,0:T(8,128)(2,1)}, u32[]{:S(2)}, u32[]{:S(2)}) async-start(bf16[4,64,2,2048]{3,1,2,0:T(8,128)(2,1)} %copy.87), calls=%async_computation.5 | async-start | bytes 4194304 | tf_op jit(solution)/shard_map/all_to_all | solution.py:119
  236.8 3.0 copy-start.6
  236.8 120.4 %reduce-scatter.3.cloned.1.call-start = ((), (), s32[]{:S(2)}) async-start(), calls=%async_computation.15 | async-start | bytes 2621440 | tf_op jit(solution)/shard_map/reduce_scatter | solution.py:194
  237.3 2.5 copy-start.1
  270.2 14.0 %copy-start.16 = (bf16[2048]{0:T(1024)(128)(2,1)S(1)}, bf16[2048]{0:T(1024)(128)(2,1)}, u32[]{:S(2)}) copy-start(bf16[2048]{0:T(1024)(128)(2,1)} %param.21) | copy-start | bytes 12292
  270.2 14.1 %copy-start.3 = (bf16[128,2048]{1,0:T(8,128)(2,1)S(1)}, bf16[128,2048]{1,0:T(8,128)(2,1)}, u32[]{:S(2)}) copy-start(bf16[128,2048]{1,0:T(8,128)(2,1)} %param.11) | copy-start | bytes 1572868
  270.2 63.6 %all-to-all-start.5 = ((bf16[4,64,2,2048]{3,0,2,1:T(4,128)(2,1)}), bf16[4,64,2,2048]{3,0,2,1:T(4,128)(2,1)}, u32[]{:S(2)}, u32[]{:S(2)}) async-start(bf16[4,64,2,2048]{3,0,2,1:T(4,128)(2,1)} %copy.88), calls=%async_computation.6 | async-start | bytes 4194304 | tf_op jit(solution)/shard_map/all_to_all | solution.py:118
  333.8 35.4 %all-to-all-start.10 = ((bf16[4,64,2]{1,2,0:T(2,128)(2,1)}), bf16[4,64,2]{1,2,0:T(2,128)(2,1)S(1)}, u32[]{:S(2)}, u32[]{:S(2)}) async-start(bf16[4,64,2]{1,2,0:T(2,128)(2,1)} %copy.95), calls=%async_computation.12 | async-start | bytes 4096 | tf_op jit(solution)/shard_map/all_to_all | solution.py:161
  337.0 91.4 %all-gather.5.cloned.1.call-start = ((), (), s32[]{:S(2)}) async-start(), calls=%async_computation.16 | async-start | bytes 2621440 | tf_op jit(solution)/shard_map/all_gather | solution.py:202
  362.6 1.9 copy-start.18
  362.6 2.2 copy-start.20
  369.2 43.9 %all-to-all-start.8 = ((bf16[4,64,2,2048]{3,1,2,0:T(8,128)(2,1)}), bf16[4,64,2,2048]{3,1,2,0:T(8,128)(2,1)}, u32[]{:S(2)}, u32[]{:S(2)}) async-start(bf16[4,64,2,2048]{3,1,2,0:T(8,128)(2,1)} %copy.92), calls=%async_computation.10 | async-start | bytes 4194304 | tf_op jit(solution)/shard_map/all_to_all | solution.py:148
  413.1 20.4 %all-to-all-start.11 = ((bf16[4,64,2]{0,2,1:T(2,128)(2,1)}), bf16[4,64,2]{0,2,1:T(2,128)(2,1)S(1)}, u32[]{:S(2)}, u32[]{:S(2)}) async-start(bf16[4,64,2]{0,2,1:T(2,128)(2,1)} %copy.96), calls=%async_computation.13 | async-start | bytes 65536 | tf_op jit(solution)/shard_map/all_to_all | solution.py:160
  423.8 4.7 copy-start.11
  428.4 2.4 copy-start.5
  428.4 2.4 copy-start.13
  433.5 10.9 %copy-start.7 = (bf16[2048,128]{1,0:T(8,128)(2,1)S(1)}, bf16[2048,128]{1,0:T(8,128)(2,1)}, u32[]{:S(2)}) copy-start(bf16[2048,128]{1,0:T(8,128)(2,1)} %param.19) | copy-start | bytes 1572868
  433.5 60.2 %all-to-all-start.9 = ((bf16[4,64,2,2048]{3,0,2,1:T(4,128)(2,1)}), bf16[4,64,2,2048]{3,0,2,1:T(4,128)(2,1)}, u32[]{:S(2)}, u32[]{:S(2)}) async-start(bf16[4,64,2,2048]{3,0,2,1:T(4,128)(2,1)} %copy.93), calls=%async_computation.11 | async-start | bytes 4194304 | tf_op jit(solution)/shard_map/all_to_all | solution.py:147
  444.1 69.5 %reduce-scatter.5.cloned.1.call-start = ((), (), s32[]{:S(2)}) async-start(), calls=%async_computation.17 | async-start | bytes 2621440 | tf_op jit(solution)/shard_map/reduce_scatter | solution.py:210
  (4 other events, 5.2 us)
Sparse Core Ops, SparseCore 0:
  179.3 32.4 all-gather.2
  243.4 38.1 reduce-scatter.2
  359.8 43.5 all-gather.4
  448.9 31.5 reduce-scatter.4
where the time goes:
time: 533 us; the launch traced here: 523 us
  waiting for transfers between devices  272 us (51%)
  local copies, waits for them, and re-layouts  92.2 us (17%)
  starting transfers between devices  90.9 us (17%)
  matrix products  23.8 us (4%)
  other arithmetic  19.9 us (4%)
  between operations  14.8 us (3%)
  blocking collectives  8.75 us (2%)
    all_to_all x1, waiting for transfers between devices, local(): lax.all_to_all(lax.all_to_all(routed.reshape(layout + (model_width,)), 't...  48.6 us
    all_to_all x1, waiting for transfers between devices, local(): lax.all_to_all(lax.all_to_all(send_rows.reshape(layout + (model_width,)),...  44.2 us
    all_to_all x1, waiting for transfers between devices, local(): lax.all_to_all(lax.all_to_all(send_cot.reshape(layout + (model_width,)),...  41.9 us
    all_to_all x1, waiting for transfers between devices, local(): lax.all_to_all(lax.all_to_all(input_grad.reshape(layout + (model_width,))...  41.9 us
    all_to_all x1, waiting for transfers between devices, local(): lax.all_to_all(input_grad.reshape(layout + (model_width,)), 'tp', split_a...  38.7 us
    all_to_all x1, waiting for transfers between devices, local(): lax.all_to_all(routed.reshape(layout + (model_width,)), 'tp', split_axis=...  22.4 us
    all_to_all x1, waiting for transfers between devices, local(): lax.all_to_all(send_cot.reshape(layout + (model_width,)), 'tp', split_axi...  19.7 us
    all_to_all x1, waiting for transfers between devices, local(): lax.all_to_all(send_rows.reshape(layout + (model_width,)), 'tp', split_ax...  14.3 us
  transfers between devices with their start and end apart: 15, of which 8 were waited for; matrix products, arithmetic and copies ran while one was open for 24% of the time, Pallas kernels for 0%

commit v1 on v0

v1 whole, which is shorter than its diff:
```python
import jax
import jax.numpy as jnp
from jax import lax
from jax.experimental import pallas as pl
from jax.experimental.pallas import tpu as pltpu
from jax.sharding import PartitionSpec as P

AXES = ("tp", "ep")
LANES = 128
TILE = 16
VMEM = pltpu.VMEM
SMEM = pltpu.SMEM


def silu_grad(argument):
    gate_sig = jax.nn.sigmoid(argument)
    return gate_sig * (1.0 + argument * (1.0 - gate_sig))


def swap_matrix():
    size = TILE * TILE
    row = lax.broadcasted_iota(jnp.int32, (size, size), 0)
    col = lax.broadcasted_iota(jnp.int32, (size, size), 1)
    return jnp.where(((row & 15) * 16 + (row >> 4)) == col, 1.0, 0.0).astype(jnp.bfloat16)


def swap(perm, block):
    return jnp.dot(perm, block, preferred_element_type=jnp.float32).astype(jnp.bfloat16)


def columns_stacked(block):
    return jnp.concatenate(
        [block[:, j * LANES : (j + 1) * LANES] for j in range(TILE)], axis=0
    )


def rows_from_stack(stack):
    return jnp.concatenate([stack[j * TILE : (j + 1) * TILE] for j in range(TILE)], axis=1)


def pack_kernel(slot_ref, weight_ref, tokens_ref, cot_ref, out_ref, token_tiles, cot_tiles):
    perm = swap_matrix()
    count = tokens_ref.shape[0]
    zero = jnp.zeros((TILE, TILE, LANES), jnp.bfloat16)

    def clear(step, carry):
        out_ref[pl.ds(step * TILE, TILE)] = zero
        return carry

    lax.fori_loop(0, out_ref.shape[0] // TILE, clear, 0)
    for group in range(count // TILE):
        rows = slice(group * TILE, (group + 1) * TILE)
        both = jnp.concatenate(
            [columns_stacked(tokens_ref[rows, :]), columns_stacked(cot_ref[rows, :])], axis=1
        )
        both = swap(perm, both)
        token_tiles[rows] = both[:, :LANES].reshape(TILE, TILE, LANES)
        cot_tiles[rows] = both[:, LANES:].reshape(TILE, TILE, LANES)

    def place(token, carry):
        row = token_tiles[token]
        cot = cot_tiles[token].astype(jnp.float32)
        for k in range(2):
            slot = slot_ref[2 * token + k]
            at = (slot >> 1) * 4 + (slot & 1)
            out_ref[at] = row
            out_ref[at + 2] = (weight_ref[2 * token + k] * cot).astype(jnp.bfloat16)
        return carry

    lax.fori_loop(0, count, place, 0, unroll=4)


def pack(slots, weights, tokens, cot):
    count = tokens.shape[0]
    return pl.pallas_call(
        pack_kernel,
        out_shape=jax.ShapeDtypeStruct((1024, TILE, LANES), jnp.bfloat16),
        in_specs=[pl.BlockSpec(memory_space=SMEM)] * 2 + [pl.BlockSpec(memory_space=VMEM)] * 2,
        out_specs=pl.BlockSpec(memory_space=VMEM),
        scratch_shapes=[pltpu.VMEM((count, TILE, LANES), jnp.bfloat16)] * 2,
        compiler_params=pltpu.CompilerParams(vmem_limit_bytes=32 << 20),
        cost_estimate=pl.CostEstimate(
            flops=8 * 2 * 256**3, bytes_accessed=5 << 20, transcendentals=0
        ),
    )(slots, weights, tokens, cot)


def expert_kernel(got_ref, gate_ref, up_ref, down_ref, back_ref, rows, cots, outs, grads):
    perm = swap_matrix()
    count = rows.shape[0]

    def load(group, carry):
        tiles = got_ref[pl.ds(group * 32, 32)].reshape(8, 2, 2, TILE, LANES)
        both = jnp.concatenate(
            [tiles[:, 0].reshape(256, LANES), tiles[:, 1].reshape(256, LANES)], axis=1
        )
        both = swap(perm, both)
        at = pl.ds(pl.multiple_of(group * TILE, TILE), TILE)
        rows[at, :] = rows_from_stack(both[:, :LANES])
        cots[at, :] = rows_from_stack(both[:, LANES:])
        return carry

    lax.fori_loop(0, count // TILE, load, 0, unroll=2)
    one = (((1,), (0,)), ((), ()))
    other = (((1,), (1,)), ((), ()))

    def dot(a, b, dims):
        return lax.dot_general(a, b, dims, preferred_element_type=jnp.float32)

    pre_gate = dot(rows[...], gate_ref[...], one)
    pre_up = dot(rows[...], up_ref[...], one)
    sig = 1.0 / (1.0 + jnp.exp(-pre_gate))
    silu = pre_gate * sig
    hidden = (silu * pre_up).astype(jnp.bfloat16)
    outs[...] = dot(hidden, down_ref[...], one).astype(jnp.bfloat16)
    hidden_grad = dot(cots[...], down_ref[...], other)
    gate_part = (hidden_grad * pre_up * (sig * (1.0 + pre_gate * (1.0 - sig)))).astype(jnp.bfloat16)
    up_part = (hidden_grad * silu).astype(jnp.bfloat16)
    grads[...] = (dot(gate_part, gate_ref[...], other) + dot(up_part, up_ref[...], other)).astype(
        jnp.bfloat16
    )

    def store(group, carry):
        at = pl.ds(pl.multiple_of(group * TILE, TILE), TILE)
        both = jnp.concatenate(
            [columns_stacked(outs[at, :]), columns_stacked(grads[at, :])], axis=1
        )
        both = swap(perm, both)
        tiles = jnp.concatenate(
            [
                both[:, :LANES].reshape(8, 1, 2, TILE, LANES),
                both[:, LANES:].reshape(8, 1, 2, TILE, LANES),
            ],
            axis=1,
        )
        back_ref[pl.ds(group * 32, 32)] = tiles.reshape(32, TILE, LANES)
        return carry

    lax.fori_loop(0, count // TILE, store, 0, unroll=2)


def expert(got, gate, up, down):
    width, units = gate.shape
    steps = 2
    count = got.shape[0] // 2 // steps
    block = pl.BlockSpec((got.shape[0] // steps, TILE, LANES), lambda i: (i, 0, 0))

    def whole(array):
        return pl.BlockSpec(array.shape, lambda i: (0, 0), pipeline_mode=pl.Buffered(1))

    return pl.pallas_call(
        expert_kernel,
        out_shape=jax.ShapeDtypeStruct(got.shape, jnp.bfloat16),
        grid=(steps,),
        in_specs=[block, whole(gate), whole(up), whole(down)],
        out_specs=block,
        scratch_shapes=[pltpu.VMEM((count, width), jnp.bfloat16)] * 4,
        compiler_params=pltpu.CompilerParams(vmem_limit_bytes=50 << 20),
        cost_estimate=pl.CostEstimate(
            flops=512 * 2048 * 512 * 12, bytes_accessed=14 << 20, transcendentals=512 * 512
        ),
    )(got, gate, up, down)


def combine_kernel(
    slot_ref,
    weight_ref,
    rows_ref,
    cot_ref,
    shared_ref,
    shared_grad_ref,
    mixed_ref,
    grad_ref,
    gate_ref,
    mixed_tiles,
    grad_tiles,
    partial,
):
    perm = swap_matrix()
    count = cot_ref.shape[0]

    def gather(token, carry):
        cot = cot_ref[token].astype(jnp.float32)
        mixed = shared_ref[token]
        grad = shared_grad_ref[token]
        for k in range(2):
            slot = slot_ref[2 * token + k]
            at = (slot >> 1) * 4 + (slot & 1)
            output = rows_ref[at].astype(jnp.float32)
            mixed = mixed + weight_ref[2 * token + k] * output
            grad = grad + rows_ref[at + 2].astype(jnp.float32)
            partial[k, token] = jnp.sum((cot * output).reshape(2, 8, LANES), axis=0)
        mixed_tiles[token] = mixed.astype(jnp.bfloat16)
        grad_tiles[token] = grad.astype(jnp.bfloat16)
        return carry

    lax.fori_loop(0, count, gather, 0, unroll=4)
    for group in range(count // TILE):
        at = slice(group * TILE, (group + 1) * TILE)
        both = jnp.concatenate(
            [mixed_tiles[at].reshape(256, LANES), grad_tiles[at].reshape(256, LANES)], axis=1
        )
        both = swap(perm, both)
        mixed_ref[at, :] = rows_from_stack(both[:, :LANES])
        grad_ref[at, :] = rows_from_stack(both[:, LANES:])
    for k in range(2):
        gate_ref[:, k : k + 1] = jnp.sum(jnp.sum(partial[k], axis=1), axis=1, keepdims=True)


def combine(slots, weights, rows, cot, shared, shared_grad):
    count = cot.shape[0]
    width = TILE * LANES
    return pl.pallas_call(
        combine_kernel,
        out_shape=[
            jax.ShapeDtypeStruct((count, width), jnp.bfloat16),
            jax.ShapeDtypeStruct((count, width), jnp.bfloat16),
            jax.ShapeDtypeStruct((count, 2), jnp.float32),
        ],
        in_specs=[pl.BlockSpec(memory_space=SMEM)] * 2 + [pl.BlockSpec(memory_space=VMEM)] * 4,
        out_specs=[pl.BlockSpec(memory_space=VMEM)] * 3,
        scratch_shapes=[
            pltpu.VMEM((count, TILE, LANES), jnp.bfloat16),
            pltpu.VMEM((count, TILE, LANES), jnp.bfloat16),
            pltpu.VMEM((2, count, 8, LANES), jnp.float32),
        ],
        compiler_params=pltpu.CompilerParams(vmem_limit_bytes=32 << 20),
        cost_estimate=pl.CostEstimate(
            flops=8 * 2 * 256**3, bytes_accessed=8 << 20, transcendentals=0
        ),
    )(slots, weights, rows, cot, shared, shared_grad)


def route_slots(expert_ids):
    chosen = expert_ids.reshape(-1)
    number = jnp.arange(chosen.shape[0], dtype=jnp.int32)
    same = (chosen[:, None] == chosen[None, :]) & (number[None, :] < number[:, None])
    return chosen * 2 + jnp.sum(same.astype(jnp.int32), axis=1)


def shared_expert(tokens, grad_out, gate, up, down, switch_vector):
    def dot(a, b, spec):
        return jnp.einsum(spec, a, b, preferred_element_type=jnp.float32)

    switch = jax.nn.sigmoid(jnp.dot(tokens, switch_vector, preferred_element_type=jnp.float32))
    pre_gate = dot(tokens, gate, "td,df->tf")
    pre_up = dot(tokens, up, "td,df->tf")
    hidden = (jax.nn.silu(pre_gate) * pre_up).astype(jnp.bfloat16)
    shared = dot(hidden, down, "tf,fd->td")
    cot = grad_out.astype(jnp.float32)
    shared_cot = (switch[:, None] * cot).astype(jnp.bfloat16)
    hidden_grad = dot(shared_cot, down, "td,fd->tf")
    gate_part = (hidden_grad * pre_up * silu_grad(pre_gate)).astype(jnp.bfloat16)
    up_part = (hidden_grad * jax.nn.silu(pre_gate)).astype(jnp.bfloat16)
    input_grad = dot(gate_part, gate, "tf,df->td") + dot(up_part, up, "tf,df->td")
    switch_grad = switch * (1.0 - switch) * jnp.sum(cot * shared, axis=1)
    grad = input_grad + switch_grad[:, None] * switch_vector.astype(jnp.float32)[None, :]
    return switch[:, None] * shared, grad


def local(
    tokens,
    expert_ids,
    gate_weights,
    grad_out,
    expert_gate,
    expert_up,
    expert_down,
    shared_gate,
    shared_up,
    shared_down,
    shared_switch,
):
    devices = lax.axis_size("tp") * lax.axis_size("ep")
    tiled = (tokens.shape[0], TILE, LANES)
    slots = route_slots(expert_ids)
    weights = gate_weights.reshape(-1)
    sent = pack(slots, weights, tokens, grad_out)

    def exchange(rows):
        return lax.all_to_all(
            rows.reshape(devices, -1, LANES), AXES, split_axis=0, concat_axis=0, tiled=True
        ).reshape(rows.shape)

    got = exchange(sent)
    all_gate = lax.all_gather(shared_gate, "tp", axis=1, tiled=True)
    all_up = lax.all_gather(shared_up, "tp", axis=1, tiled=True)
    all_down = lax.all_gather(shared_down, "tp", axis=0, tiled=True)
    back = exchange(expert(got, expert_gate[0], expert_up[0], expert_down[0]))
    shared, shared_grad = shared_expert(
        tokens, grad_out, all_gate, all_up, all_down, shared_switch
    )
    mixed, grad_tokens, gate_grad = combine(
        slots,
        weights,
        back,
        grad_out.reshape(tiled),
        shared.reshape(tiled),
        shared_grad.reshape(tiled),
    )
    return (mixed, grad_tokens, gate_grad)


def solution(mesh):
    rows = P(AXES, None)
    experts = P(AXES, None, None)
    placed = (rows, rows, rows, rows, experts, experts, experts)
    placed += (P(None, "tp"), P(None, "tp"), P("tp", None), P())
    return jax.shard_map(
        local, mesh=mesh, in_specs=placed, out_specs=(rows, rows, rows), check_vma=False
    )
```

time: 533 us -> 279 us (0.52); the launches traced: 523 us -> 278 us
  local copies, waits for them, and re-layouts: 92.2 us -> 8.5 us
  waiting for transfers between devices: 272 us -> 195 us
  starting transfers between devices: 90.9 us -> 24.5 us
  Pallas kernels: 0 us -> 26.6 us
  other arithmetic: 19.9 us -> 0.2 us
  matrix products: 23.8 us -> 9.2 us
  blocking collectives: 8.75 us -> 0 us
    all_to_all x11 -> x2, waiting for transfers between devices: 272 us -> 96.6 us  [exchange(): lax.all_to_all(rows.reshape(devices, -1, LANES), AXES, split_axis=0, conc...]
    all_gather x2 -> x3, waiting for transfers between devices: 0.02 us -> 96.7 us  [the longest x1 53.3 us: local(): all_up = lax.all_gather(shared_up, 'tp', axis=1, tiled=True)]
    all_to_all x11 -> x2, starting transfers between devices: 90.1 us -> 24.4 us  [exchange(): lax.all_to_all(rows.reshape(devices, -1, LANES), AXES, split_axis=0, conc...]
    all_to_all x11 -> x0, local copies, waits for them, and re-layouts: 34.9 us -> none  [the longest x1 5.45 us: local(): lax.all_to_all(send_rows.reshape(layout + (model_width,)), 'tp', split_ax...]
    pallas_call x0 -> x3, Pallas kernels: none -> 26.6 us  [the longest x1 19.5 us: expert(): pl.pallas_call(expert_kernel, out_shape=jax.ShapeDtypeStruct(got.shape, j...]
    reshape x12 -> x2, local copies, waits for them, and re-layouts: 23.4 us -> 0.27 us  [the longest x1 0.14 us: route_slots(): chosen = expert_ids.reshape(-1)]
    dot_general x13 -> x7, matrix products: 23.8 us -> 9.2 us  [the longest x6 8.96 us: dot(): return jnp.einsum(spec, a, b, preferred_element_type=jnp.float32)]
    reduce_sum x4 -> x1, other arithmetic: 11 us -> 0.18 us  [route_slots(): return chosen * 2 + jnp.sum(same.astype(jnp.int32), axis=1)]
  transfers between devices with their start and end apart: 15 -> 5, of which waited for: 8 -> 3; matrix products, arithmetic and copies ran while one was open for 24% -> 3% of each run, Pallas kernels for 0% -> 7%
where the time goes in v1:
time: 279 us; the launch traced here: 278 us
  waiting for transfers between devices  195 us (70%)
  Pallas kernels  26.6 us (10%)
  starting transfers between devices  24.5 us (9%)
  between operations  13.9 us (5%)
  matrix products  9.2 us (3%)
  local copies, waits for them, and re-layouts  8.5 us (3%)
    all_to_all x2, waiting for transfers between devices, exchange(): lax.all_to_all(rows.reshape(devices, -1, LANES), AXES, split_axis=0, conc...  96.6 us
    all_gather x1, waiting for transfers between devices, local(): all_up = lax.all_gather(shared_up, 'tp', axis=1, tiled=True)  53.3 us
    all_gather x1, waiting for transfers between devices, local(): all_down = lax.all_gather(shared_down, 'tp', axis=0, tiled=True)  43.4 us
    all_to_all x2, starting transfers between devices, exchange(): lax.all_to_all(rows.reshape(devices, -1, LANES), AXES, split_axis=0, conc...  24.4 us
    pallas_call x1, Pallas kernels, expert(): pl.pallas_call(expert_kernel, out_shape=jax.ShapeDtypeStruct(got.shape, j...  19.5 us
    dot_general x6, matrix products, dot(): return jnp.einsum(spec, a, b, preferred_element_type=jnp.float32)  8.96 us
    unnamed x26, local copies, waits for them, and re-layouts  7.6 us
  transfers between devices with their start and end apart: 5, of which 3 were waited for; matrix products, arithmetic and copies ran while one was open for 3% of the time, Pallas kernels for 7%

profile of v1, /device:TPU:1, one launch (start us, length us, event | category | flops | bytes accessed | tf_op | source)
XLA Modules:
  0.0 278.4 jit_solution(7939217179705064731)
XLA Ops:
  7.2 0.8 copy.18
  8.0 0.1 reshape.38
  8.1 0.2 convert_reduce_fusion
  8.3 0.8 copy.19
  9.1 0.1 reshape.39.weight_ref
  9.2 1.0 copy-done.1
  10.3 1.0 copy-done.3
  11.3 2.5 shard_map.130
  13.8 1.9 copy-done
  15.7 16.7 %all-to-all-start = ((bf16[256,64,128]{2,1,0:T(8,128)(2,1)}), bf16[256,64,128]{2,1,0:T(8,128)(2,1)}, u32[]{:S(2)}, u32[]{:S(2)}) async-start(bf16[256,64,128]{2,1,0:T(8,128)(2,1)} %bitcast.35), calls=%async_computation | async-start | bytes 8388608 | tf_op jit(solution)/shard_map/all_to_all | solution.py:281
  32.4 0.7 all-gather.4.cloned.1.call-update
  33.1 96.6 %all-to-all-done = bf16[256,64,128]{2,1,0:T(8,128)(2,1)} async-done(((bf16[256,64,128]{2,1,0:T(8,128)(2,1)}), bf16[256,64,128]{2,1,0:T(8,128)(2,1)}, u32[]{:S(2)}, u32[]{:S(2)}) %all-to-all-start) | async-done | bytes 4194336 | tf_op jit(solution)/shard_map/all_to_all | solution.py:281
  129.7 19.5 %shard_map.131 = bf16[1024,16,128]{2,1,0:T(8,128)(2,1)} custom-call(bf16[1024,16,128]{2,1,0:T(8,128)(2,1)} %bitcast.1.got_ref, bf16[2048,512]{1,0:T(8,128)(2,1)S(1)} %bitcast.40, bf16[2048,512]{1,0:T(8,128)(2,1)} %bitcast.42, bf16[512,2048]{1,0:T(8,128)(2,1)} %bitcast.43), custom_call_target="tpu_custom_call" | custom-call | flops 6442450944 | bytes 14680064 | tf_op jit(solution)/shard_map/pallas_call | solution.py:151
  149.2 7.8 %all-to-all-start.1 = ((bf16[256,64,128]{2,1,0:T(8,128)(2,1)}), bf16[256,64,128]{2,1,0:T(8,128)(2,1)}, u32[]{:S(2)}, u32[]{:S(2)}) async-start(bf16[256,64,128]{2,1,0:T(8,128)(2,1)} %bitcast.41), calls=%async_computation.1 | async-start | bytes 8388608 | tf_op jit(solution)/shard_map/all_to_all | solution.py:281
  157.1 0.7 all-gather.6.cloned.1.call-update
  157.8 0.7 all-gather.8.cloned.1.call-update
  158.5 0.1 copy.21
  158.7 0.2 fusion.5
  158.9 2.1 fusion.22
  161.0 53.3 %all-gather.6.cloned.1.call-done = bf16[2048,512]{1,0:T(8,128)(2,1)} async-done(((bf16[2048,128]{1,0:T(8,128)(2,1)}), bf16[2048,512]{1,0:T(8,128)(2,1)}) %all-gather.6.cloned.1.call-update) | async-done | bytes 2097168 | tf_op jit(solution)/shard_map/all_gather | solution.py:287
  214.3 2.0 fusion.23
  216.3 43.4 %all-gather.8.cloned.1.call-done = bf16[512,2048]{1,0:T(8,128)(2,1)} async-done(((bf16[128,2048]{1,0:T(8,128)(2,1)}), bf16[512,2048]{1,0:T(8,128)(2,1)}) %all-gather.8.cloned.1.call-update) | async-done | bytes 2097168 | tf_op jit(solution)/shard_map/all_gather | solution.py:288
  259.8 2.4 fusion.7
  262.2 0.8 fusion.8
  263.0 0.7 copy-done.8
  263.7 0.8 fusion.14
  264.6 0.8 copy-done.7
  265.3 0.8 fusion.1
  266.2 0.2 copy.23
  266.4 0.2 copy.22
  266.6 4.7 %shard_map.132 = (bf16[128,2048]{1,0:T(8,128)(2,1)}, bf16[128,2048]{1,0:T(8,128)(2,1)}, f32[128,2]{1,0:T(8,128)S(1)}) custom-call(s32[256]{0:T(256)S(1)} %multiply_add_fusion.slot_ref, f32[256]{0:T(256)S(1)} %reshape.39.weight_ref, bf16[1024,16,128]{2,1,0:T(8,128)(2,1)} %bitcast.6.rows_ref, bf16[128,16,128]{2,1,0:T(8,128)(2,1)S(1)} %bitcast.39, ...), custom_call_target="tpu_custom_call" | custom-call | flops 268435456 | bytes 8388608 | tf_op jit(solution)/shard_map/pallas_call | solution.py:213
  271.3 0.6 copy.20
  (24 shorter events, 0.2 us)
Async XLA Ops:
  9.2 1.0 copy-start.1
  10.3 1.0 copy-start.3
  13.8 2.0 copy-start
  15.7 114.0 %copy-start.5 = (bf16[1,2048,512]{2,1,0:T(8,128)(2,1)S(1)}, bf16[1,2048,512]{2,1,0:T(8,128)(2,1)}, u32[]{:S(2)}) copy-start(bf16[1,2048,512]{2,1,0:T(8,128)(2,1)} %param.15) | copy-start | bytes 6291460
  15.7 114.0 %all-to-all-start = ((bf16[256,64,128]{2,1,0:T(8,128)(2,1)}), bf16[256,64,128]{2,1,0:T(8,128)(2,1)}, u32[]{:S(2)}, u32[]{:S(2)}) async-start(bf16[256,64,128]{2,1,0:T(8,128)(2,1)} %bitcast.35), calls=%async_computation | async-start | bytes 8388608 | tf_op jit(solution)/shard_map/all_to_all | solution.py:281
  32.4 126.5 %all-gather.4.cloned.1.call-start = ((), (), s32[]{:S(2)}) async-start(), calls=%async_computation.2 | async-start | bytes 2621440 | tf_op jit(solution)/shard_map/all_gather | solution.py:286
  149.2 9.3 %copy-start.9 = (bf16[2048]{0:T(1024)(128)(2,1)S(1)}, bf16[2048]{0:T(1024)(128)(2,1)}, u32[]{:S(2)}) copy-start(bf16[2048]{0:T(1024)(128)(2,1)} %param.21) | copy-start | bytes 12292
  149.2 9.3 %copy-start.2 = (bf16[128,2048]{1,0:T(8,128)(2,1)S(1)}, bf16[128,2048]{1,0:T(8,128)(2,1)}, u32[]{:S(2)}) copy-start(bf16[128,2048]{1,0:T(8,128)(2,1)} %cot_ref.1) | copy-start | bytes 1572868
  149.2 117.3 %all-to-all-start.1 = ((bf16[256,64,128]{2,1,0:T(8,128)(2,1)}), bf16[256,64,128]{2,1,0:T(8,128)(2,1)}, u32[]{:S(2)}, u32[]{:S(2)}) async-start(bf16[256,64,128]{2,1,0:T(8,128)(2,1)} %bitcast.41), calls=%async_computation.1 | async-start | bytes 8388608 | tf_op jit(solution)/shard_map/all_to_all | solution.py:281
  157.0 1.7 copy-start.4
  157.0 57.3 %all-gather.6.cloned.1.call-start = ((), (), s32[]{:S(2)}) async-start(), calls=%async_computation.3 | async-start | bytes 2621440 | tf_op jit(solution)/shard_map/all_gather | solution.py:287
  157.8 102.0 %all-gather.8.cloned.1.call-start = ((), (), s32[]{:S(2)}) async-start(), calls=%async_computation.4 | async-start | bytes 2621440 | tf_op jit(solution)/shard_map/all_gather | solution.py:288
  259.8 2.4 copy-start.6
  262.1 1.6 copy-start.8
  263.7 1.6 copy-start.7
Sparse Core Ops, SparseCore 0:
  35.0 54.3 all-gather.3
  159.7 54.5 all-gather.5
  216.1 43.6 all-gather.7

commit v2 on v1

--- a/solution.py
+++ b/solution.py
@@ -61,10 +61,10 @@
         row = token_tiles[token]
         cot = cot_tiles[token].astype(jnp.float32)
         for k in range(2):
-            slot = slot_ref[2 * token + k]
+            slot = slot_ref[k * count + token]
             at = (slot >> 1) * 4 + (slot & 1)
             out_ref[at] = row
-            out_ref[at + 2] = (weight_ref[2 * token + k] * cot).astype(jnp.bfloat16)
+            out_ref[at + 2] = (weight_ref[k * count + token] * cot).astype(jnp.bfloat16)
         return carry
 
     lax.fori_loop(0, count, place, 0, unroll=4)
@@ -85,9 +85,33 @@
     )(slots, weights, tokens, cot)
 
 
-def expert_kernel(got_ref, gate_ref, up_ref, down_ref, back_ref, rows, cots, outs, grads):
+def expert_kernel(
+    got_ref,
+    gate_from,
+    up_from,
+    down_from,
+    back_ref,
+    rows,
+    cots,
+    outs,
+    grads,
+    gate_ref,
+    up_ref,
+    down_ref,
+    arrived,
+):
     perm = swap_matrix()
     count = rows.shape[0]
+    copies = [
+        pltpu.make_async_copy(gate_from, gate_ref, arrived.at[0]),
+        pltpu.make_async_copy(up_from, up_ref, arrived.at[1]),
+        pltpu.make_async_copy(down_from, down_ref, arrived.at[2]),
+    ]
+
+    @pl.when(pl.program_id(0) == 0)
+    def _():
+        for copy in copies:
+            copy.start()
 
     def load(group, carry):
         tiles = got_ref[pl.ds(group * 32, 32)].reshape(8, 2, 2, TILE, LANES)
@@ -100,7 +124,13 @@
         cots[at, :] = rows_from_stack(both[:, LANES:])
         return carry
 
-    lax.fori_loop(0, count // TILE, load, 0, unroll=2)
+    lax.fori_loop(0, count // TILE, load, 0, unroll=True)
+
+    @pl.when(pl.program_id(0) == 0)
+    def _():
+        for copy in copies:
+            copy.wait()
+
     one = (((1,), (0,)), ((), ()))
     other = (((1,), (1,)), ((), ()))
 
@@ -136,7 +166,7 @@
         back_ref[pl.ds(group * 32, 32)] = tiles.reshape(32, TILE, LANES)
         return carry
 
-    lax.fori_loop(0, count // TILE, store, 0, unroll=2)
+    lax.fori_loop(0, count // TILE, store, 0, unroll=True)
 
 
 def expert(got, gate, up, down):
@@ -145,21 +175,21 @@
     count = got.shape[0] // 2 // steps
     block = pl.BlockSpec((got.shape[0] // steps, TILE, LANES), lambda i: (i, 0, 0))
 
-    def whole(array):
-        return pl.BlockSpec(array.shape, lambda i: (0, 0), pipeline_mode=pl.Buffered(1))
-
+    weights = [gate, up, down]
     return pl.pallas_call(
         expert_kernel,
         out_shape=jax.ShapeDtypeStruct(got.shape, jnp.bfloat16),
         grid=(steps,),
-        in_specs=[block, whole(gate), whole(up), whole(down)],
+        in_specs=[block] + [pl.BlockSpec(memory_space=pl.ANY)] * 3,
         out_specs=block,
-        scratch_shapes=[pltpu.VMEM((count, width), jnp.bfloat16)] * 4,
+        scratch_shapes=[pltpu.VMEM((count, width), jnp.bfloat16)] * 4
+        + [pltpu.VMEM(w.shape, jnp.bfloat16) for w in weights]
+        + [pltpu.SemaphoreType.DMA((3,))],
         compiler_params=pltpu.CompilerParams(vmem_limit_bytes=50 << 20),
         cost_estimate=pl.CostEstimate(
             flops=512 * 2048 * 512 * 12, bytes_accessed=14 << 20, transcendentals=512 * 512
         ),
-    )(got, gate, up, down)
+    )(got, *weights)
 
 
 def combine_kernel(
@@ -184,10 +214,10 @@
         mixed = shared_ref[token]
         grad = shared_grad_ref[token]
         for k in range(2):
-            slot = slot_ref[2 * token + k]
+            slot = slot_ref[k * count + token]
             at = (slot >> 1) * 4 + (slot & 1)
             output = rows_ref[at].astype(jnp.float32)
-            mixed = mixed + weight_ref[2 * token + k] * output
+            mixed = mixed + weight_ref[k * count + token] * output
             grad = grad + rows_ref[at + 2].astype(jnp.float32)
             partial[k, token] = jnp.sum((cot * output).reshape(2, 8, LANES), axis=0)
         mixed_tiles[token] = mixed.astype(jnp.bfloat16)
@@ -232,7 +262,7 @@
 
 
 def route_slots(expert_ids):
-    chosen = expert_ids.reshape(-1)
+    chosen = expert_ids.T.reshape(-1)
     number = jnp.arange(chosen.shape[0], dtype=jnp.int32)
     same = (chosen[:, None] == chosen[None, :]) & (number[None, :] < number[:, None])
     return chosen * 2 + jnp.sum(same.astype(jnp.int32), axis=1)
@@ -274,7 +304,7 @@
     devices = lax.axis_size("tp") * lax.axis_size("ep")
     tiled = (tokens.shape[0], TILE, LANES)
     slots = route_slots(expert_ids)
-    weights = gate_weights.reshape(-1)
+    weights = gate_weights.T.reshape(-1)
     sent = pack(slots, weights, tokens, grad_out)
 
     def exchange(rows):
@@ -283,8 +313,11 @@
         ).reshape(rows.shape)
 
     got = exchange(sent)
-    all_gate = lax.all_gather(shared_gate, "tp", axis=1, tiled=True)
-    all_up = lax.all_gather(shared_up, "tp", axis=1, tiled=True)
+    all_in = lax.all_gather(
+        jnp.concatenate([shared_gate, shared_up], axis=0), "tp", axis=1, tiled=True
+    )
+    got, all_in, shared_down = lax.optimization_barrier((got, all_in, shared_down))
+    all_gate, all_up = jnp.split(all_in, 2, axis=0)
     all_down = lax.all_gather(shared_down, "tp", axis=0, tiled=True)
     back = exchange(expert(got, expert_gate[0], expert_up[0], expert_down[0]))
     shared, shared_grad = shared_expert(

time: 279 us -> 263 us (0.943)
  waiting for transfers between devices: 195 us -> 184 us
  Pallas kernels: 26.6 us -> 22 us
    all_to_all x2, waiting for transfers between devices: 96.6 us -> 53.4 us  [exchange(): lax.all_to_all(rows.reshape(devices, -1, LANES), AXES, split_axis=0, conc...]
    all_gather x2 -> x1, waiting for transfers between devices: 53.3 us -> 83.2 us  [local(): lax.all_gather(jnp.concatenate([shared_gate, shared_up], axis=0), 'tp', a...]
    pallas_call x1, Pallas kernels: 19.5 us -> 14.8 us  [expert(): pl.pallas_call(expert_kernel, out_shape=jax.ShapeDtypeStruct(got.shape, j...]
    all_gather x1, waiting for transfers between devices: 43.4 us -> 46.6 us  [local(): all_down = lax.all_gather(shared_down, 'tp', axis=0, tiled=True)]
    unnamed x26 -> x32, local copies, waits for them, and re-layouts: 7.6 us -> 5.89 us
  transfers between devices with their start and end apart: 5 -> 4, of which waited for: 3 -> 4; matrix products, arithmetic and copies ran while one was open for 3% -> 4% of each run, Pallas kernels for 7% -> 0%
where the time goes in v2:
time: 263 us; the launch traced here: 262 us
  waiting for transfers between devices  184 us (70%)
  starting transfers between devices  24.7 us (9%)
  Pallas kernels  22 us (8%)
  between operations  14.2 us (5%)
  matrix products  8.34 us (3%)
  local copies, waits for them, and re-layouts  6.53 us (2%)
  other arithmetic  2.72 us (1%)
    all_gather x1, waiting for transfers between devices, local(): lax.all_gather(jnp.concatenate([shared_gate, shared_up], axis=0), 'tp', a...  83.2 us
    all_to_all x2, waiting for transfers between devices, exchange(): lax.all_to_all(rows.reshape(devices, -1, LANES), AXES, split_axis=0, conc...  53.4 us
    all_gather x1, waiting for transfers between devices, local(): all_down = lax.all_gather(shared_down, 'tp', axis=0, tiled=True)  46.6 us
    all_to_all x2, starting transfers between devices, exchange(): lax.all_to_all(rows.reshape(devices, -1, LANES), AXES, split_axis=0, conc...  24.5 us
    pallas_call x1, Pallas kernels, expert(): pl.pallas_call(expert_kernel, out_shape=jax.ShapeDtypeStruct(got.shape, j...  14.8 us
    dot_general x6, matrix products, dot(): return jnp.einsum(spec, a, b, preferred_element_type=jnp.float32)  8.1 us
    unnamed x32, local copies, waits for them, and re-layouts  5.89 us
  transfers between devices with their start and end apart: 4, of which 4 were waited for; matrix products, arithmetic and copies ran while one was open for 4% of the time, Pallas kernels for 0%

profile of v2, /device:TPU:1, one launch (start us, length us, event | category | flops | bytes accessed | tf_op | source)
XLA Modules:
  0.0 262.2 jit_solution(5229028179527448704)
XLA Ops:
  7.2 0.9 convert_reduce_fusion
  8.1 0.7 multiply_add_fusion.slot_ref
  8.8 1.0 copy-done.1
  9.8 1.0 copy-done.3
  10.9 0.7 copy-done.5
  11.5 2.4 shard_map.130
  14.0 2.0 copy-done
  16.0 16.7 %all-to-all-start = ((bf16[256,64,128]{2,1,0:T(8,128)(2,1)}), bf16[256,64,128]{2,1,0:T(8,128)(2,1)}, u32[]{:S(2)}, u32[]{:S(2)}) async-start(bf16[256,64,128]{2,1,0:T(8,128)(2,1)} %bitcast.42), calls=%async_computation | async-start | bytes 8388608 | tf_op jit(solution)/shard_map/all_to_all | solution.py:311
  32.7 0.0 all-gather.3.cloned.1.call-start
  32.7 1.1 pad_maximum_fusion
  33.8 83.2 %all-gather.3.cloned.1.call-done = bf16[4096,512]{1,0:T(8,128)(2,1)} async-done(((bf16[4096,128]{1,0:T(8,128)(2,1)}), bf16[4096,512]{1,0:T(8,128)(2,1)}) %all-gather.3.cloned.1.call-update) | async-done | bytes 4194320 | tf_op jit(solution)/shard_map/all_gather | solution.py:316
  117.1 13.0 %all-to-all-done = bf16[256,64,128]{2,1,0:T(8,128)(2,1)} async-done(((bf16[256,64,128]{2,1,0:T(8,128)(2,1)}), bf16[256,64,128]{2,1,0:T(8,128)(2,1)}, u32[]{:S(2)}, u32[]{:S(2)}) %all-to-all-start) | async-done | bytes 4194336 | tf_op jit(solution)/shard_map/all_to_all | solution.py:311
  130.0 14.8 %shard_map.131 = bf16[1024,16,128]{2,1,0:T(8,128)(2,1)} custom-call(bf16[1024,16,128]{2,1,0:T(8,128)(2,1)} %bitcast.7.got_ref, bf16[2048,512]{1,0:T(8,128)(2,1)S(1)} %bitcast.49, bf16[2048,512]{1,0:T(8,128)(2,1)} %bitcast.52, bf16[512,2048]{1,0:T(8,128)(2,1)} %bitcast.53), custom_call_target="tpu_custom_call" | custom-call | flops 6442450944 | bytes 14680064 | tf_op jit(solution)/shard_map/pallas_call | solution.py:179
  144.9 7.8 %all-to-all-start.1 = ((bf16[256,64,128]{2,1,0:T(8,128)(2,1)}), bf16[256,64,128]{2,1,0:T(8,128)(2,1)}, u32[]{:S(2)}, u32[]{:S(2)}) async-start(bf16[256,64,128]{2,1,0:T(8,128)(2,1)} %bitcast.50), calls=%async_computation.1 | async-start | bytes 8388608 | tf_op jit(solution)/shard_map/all_to_all | solution.py:311
  152.7 0.2 all-gather.5.cloned.1.call-start
  152.9 0.5 all-gather.5.cloned.1.call-update
  153.5 0.1 copy.21
  153.6 0.2 fusion.20
  153.8 2.5 fusion.11
  156.4 0.3 copy-done.9
  156.7 0.7 fusion.14
  157.4 46.6 %all-gather.5.cloned.1.call-done = bf16[512,2048]{1,0:T(8,128)(2,1)} async-done(((bf16[128,2048]{1,0:T(8,128)(2,1)}), bf16[512,2048]{1,0:T(8,128)(2,1)}) %all-gather.5.cloned.1.call-update) | async-done | bytes 2097168 | tf_op jit(solution)/shard_map/all_gather | solution.py:321
  204.0 2.3 fusion.22
  206.4 0.8 fusion.23
  207.1 0.3 copy-done.10
  207.5 0.9 fusion.4
  208.3 0.9 fusion.8
  209.2 0.2 copy.23
  209.4 0.2 copy.22
  209.6 40.5 %all-to-all-done.1 = bf16[256,64,128]{2,1,0:T(8,128)(2,1)} async-done(((bf16[256,64,128]{2,1,0:T(8,128)(2,1)}), bf16[256,64,128]{2,1,0:T(8,128)(2,1)}, u32[]{:S(2)}, u32[]{:S(2)}) %all-to-all-start.1) | async-done | bytes 4194336 | tf_op jit(solution)/shard_map/all_to_all | solution.py:311
  250.1 4.7 %shard_map.132 = (bf16[128,2048]{1,0:T(8,128)(2,1)}, bf16[128,2048]{1,0:T(8,128)(2,1)}, f32[128,2]{1,0:T(8,128)S(1)}) custom-call(s32[256]{0:T(256)S(1)} %multiply_add_fusion.slot_ref, f32[256]{0:T(256)S(1)} %bitcast.48, bf16[1024,16,128]{2,1,0:T(8,128)(2,1)} %bitcast.12.rows_ref, bf16[128,16,128]{2,1,0:T(8,128)(2,1)S(1)} %bitcast.46, ...), custom_call_target="tpu_custom_call" | custom-call | flops 268435456 | bytes 8388608 | tf_op jit(solution)/shard_map/pallas_call | solution.py:243
  254.8 0.6 copy.19
  (26 shorter events, 0.1 us)
Async XLA Ops:
  8.8 1.0 copy-start.1
  9.8 1.0 copy-start.3
  10.9 0.7 copy-start.5
  14.0 2.0 copy-start
  16.0 16.7 %copy-start.11 = (bf16[2048,128]{1,0:T(8,128)(2,1)S(1)}, bf16[2048,128]{1,0:T(8,128)(2,1)}, u32[]{:S(2)}) copy-start(bf16[2048,128]{1,0:T(8,128)(2,1)} %param.19) | copy-start | bytes 1572868
  16.0 16.7 %copy-start.12 = (bf16[2048,128]{1,0:T(8,128)(2,1)S(1)}, bf16[2048,128]{1,0:T(8,128)(2,1)}, u32[]{:S(2)}) copy-start(bf16[2048,128]{1,0:T(8,128)(2,1)} %param.18) | copy-start | bytes 1572868
  16.0 114.0 %all-to-all-start = ((bf16[256,64,128]{2,1,0:T(8,128)(2,1)}), bf16[256,64,128]{2,1,0:T(8,128)(2,1)}, u32[]{:S(2)}, u32[]{:S(2)}) async-start(bf16[256,64,128]{2,1,0:T(8,128)(2,1)} %bitcast.42), calls=%async_computation | async-start | bytes 8388608 | tf_op jit(solution)/shard_map/all_to_all | solution.py:311
  32.7 97.4 %copy-start.7 = (bf16[1,2048,512]{2,1,0:T(8,128)(2,1)S(1)}, bf16[1,2048,512]{2,1,0:T(8,128)(2,1)}, u32[]{:S(2)}) copy-start(bf16[1,2048,512]{2,1,0:T(8,128)(2,1)} %param.15) | copy-start | bytes 6291460
  32.7 84.4 %all-gather.3.cloned.1.call-start = ((), (), s32[]{:S(2)}) async-start(), calls=%async_computation.2 | async-start | bytes 5242880 | tf_op jit(solution)/shard_map/all_gather | solution.py:316
  144.8 8.6 %copy-start.13 = (bf16[2048]{0:T(1024)(128)(2,1)S(1)}, bf16[2048]{0:T(1024)(128)(2,1)}, u32[]{:S(2)}) copy-start(bf16[2048]{0:T(1024)(128)(2,1)} %param.21) | copy-start | bytes 12292
  144.9 8.6 %copy-start.2 = (bf16[128,2048]{1,0:T(8,128)(2,1)S(1)}, bf16[128,2048]{1,0:T(8,128)(2,1)}, u32[]{:S(2)}) copy-start(bf16[128,2048]{1,0:T(8,128)(2,1)} %cot_ref.1) | copy-start | bytes 1572868
  144.9 8.7 %copy-start.4 = (bf16[128,2048]{1,0:T(8,128)(2,1)S(1)}, bf16[128,2048]{1,0:T(8,128)(2,1)}, u32[]{:S(2)}) copy-start(bf16[128,2048]{1,0:T(8,128)(2,1)} %tokens_ref.1) | copy-start | bytes 1572868
  144.9 105.2 %all-to-all-start.1 = ((bf16[256,64,128]{2,1,0:T(8,128)(2,1)}), bf16[256,64,128]{2,1,0:T(8,128)(2,1)}, u32[]{:S(2)}, u32[]{:S(2)}) async-start(bf16[256,64,128]{2,1,0:T(8,128)(2,1)} %bitcast.50), calls=%async_computation.1 | async-start | bytes 8388608 | tf_op jit(solution)/shard_map/all_to_all | solution.py:311
  152.7 51.3 %all-gather.5.cloned.1.call-start = ((), (), s32[]{:S(2)}) async-start(), calls=%async_computation.3 | async-start | bytes 2621440 | tf_op jit(solution)/shard_map/all_gather | solution.py:321
  153.8 2.8 %copy-start.9 = (bf16[4096,512]{1,0:T(8,128)(2,1)S(1)}, bf16[4096,512]{1,0:T(8,128)(2,1)}, u32[]{:S(2)}) copy-start(bf16[4096,512]{1,0:T(8,128)(2,1)} %all-gather.3.cloned.1.call-done) | copy-start | bytes 12582916
  204.0 2.3 copy-start.8
  204.0 3.5 %copy-start.10 = (bf16[4096,512]{1,0:T(8,128)(2,1)S(1)}, bf16[4096,512]{1,0:T(8,128)(2,1)}, u32[]{:S(2)}) copy-start(bf16[4096,512]{1,0:T(8,128)(2,1)} %all-gather.3.cloned.1.call-done) | copy-start | bytes 12582916
  209.2 40.9 %copy-start.6 = (f32[128,2]{0,1:T(2,128)S(1)}, f32[128,2]{0,1:T(2,128)}, u32[]{:S(2)}) copy-start(f32[128,2]{0,1:T(2,128)} %param.13) | copy-start | bytes 3076
Sparse Core Ops, SparseCore 0:
  35.3 81.7 all-gather.2
  155.3 48.6 all-gather.4

commit v3 on v1

v3 whole, which is shorter than its diff:
```python
import jax
import jax.numpy as jnp
from jax import lax
from jax.experimental import pallas as pl
from jax.experimental.pallas import tpu as pltpu
from jax.sharding import PartitionSpec as P

AXES = ("tp", "ep")
LANES = 128
TILE = 16
VMEM = pltpu.VMEM
SMEM = pltpu.SMEM
HBM = pltpu.HBM
PARTS = 4


def silu_grad(argument):
    gate_sig = jax.nn.sigmoid(argument)
    return gate_sig * (1.0 + argument * (1.0 - gate_sig))


def swap_matrix():
    size = TILE * TILE
    row = lax.broadcasted_iota(jnp.int32, (size, size), 0)
    col = lax.broadcasted_iota(jnp.int32, (size, size), 1)
    return jnp.where(((row & 15) * 16 + (row >> 4)) == col, 1.0, 0.0).astype(jnp.bfloat16)


def swap(perm, block):
    return jnp.dot(perm, block, preferred_element_type=jnp.float32).astype(jnp.bfloat16)


def columns_stacked(block):
    return jnp.concatenate(
        [block[:, j * LANES : (j + 1) * LANES] for j in range(TILE)], axis=0
    )


def rows_from_stack(stack):
    return jnp.concatenate([stack[j * TILE : (j + 1) * TILE] for j in range(TILE)], axis=1)


def pack_kernel(
    chosen_ref, weight_ref, tokens_from, cot_from, out_ref, tokens, cots, token_tiles, cot_tiles,
    first, second, moved
):
    came = [
        pltpu.make_async_copy(tokens_from, tokens, moved.at[0]),
        pltpu.make_async_copy(cot_from, cots, moved.at[1]),
    ]
    for copy in came:
        copy.start()
    perm = swap_matrix()
    count = tokens.shape[0]
    zero = jnp.zeros((8, 2, TILE, LANES), jnp.bfloat16)

    def clear(step, carry):
        first[pl.ds(step * 8, 8)] = zero
        second[pl.ds(step * 8, 8)] = zero
        return carry

    lax.fori_loop(0, first.shape[0] // 8, clear, 0, unroll=4)
    for copy in came:
        copy.wait()
    for group in range(count // TILE):
        rows = slice(group * TILE, (group + 1) * TILE)
        both = jnp.concatenate(
            [columns_stacked(tokens[rows, :]), columns_stacked(cots[rows, :])], axis=1
        )
        both = swap(perm, both)
        token_tiles[rows] = both[:, :LANES].reshape(TILE, TILE, LANES)
        cot_tiles[rows] = both[:, LANES:].reshape(TILE, TILE, LANES)

    def place(slot, order, backward):
        def step(number, carry):
            token = count - 1 - number if backward else number
            row = token_tiles[token]
            cot = cot_tiles[token].astype(jnp.float32)
            for k in order:
                at = chosen_ref[k * count + token]
                slot[at, 0] = row
                slot[at, 1] = (weight_ref[k * count + token] * cot).astype(jnp.bfloat16)
            return carry

        lax.fori_loop(0, count, step, 0, unroll=4)

    gone = [
        pltpu.make_async_copy(first, out_ref.at[:, 0], moved.at[2]),
        pltpu.make_async_copy(second, out_ref.at[:, 1], moved.at[3]),
    ]
    place(first, (0, 1), False)
    gone[0].start()
    place(second, (1, 0), True)
    gone[1].start()
    for copy in gone:
        copy.wait()


def pack(chosen, weights, tokens, cot, experts):
    count = tokens.shape[0]
    return pl.pallas_call(
        pack_kernel,
        out_shape=jax.ShapeDtypeStruct((experts, 2, 2, TILE, LANES), jnp.bfloat16),
        in_specs=[pl.BlockSpec(memory_space=SMEM)] * 2 + [pl.BlockSpec(memory_space=HBM)] * 2,
        out_specs=pl.BlockSpec(memory_space=HBM),
        scratch_shapes=[pltpu.VMEM(tokens.shape, jnp.bfloat16)] * 2
        + [pltpu.VMEM((count, TILE, LANES), jnp.bfloat16)] * 2
        + [pltpu.VMEM((experts, 2, TILE, LANES), jnp.bfloat16)] * 2
        + [pltpu.SemaphoreType.DMA((4,))],
        compiler_params=pltpu.CompilerParams(vmem_limit_bytes=32 << 20),
        cost_estimate=pl.CostEstimate(
            flops=8 * 2 * 256**3, bytes_accessed=5 << 20, transcendentals=0
        ),
    )(chosen, weights, tokens, cot)


def expert_kernel(
    got_from, gate_from, up_from, down_from, back_to, got, back, rows, cots, outs, grads, gate_ref,
    up_ref, down_ref, arrived, came, gone
):
    perm = swap_matrix()
    blocks, count, width = rows.shape
    weights = [
        pltpu.make_async_copy(gate_from, gate_ref, arrived.at[0]),
        pltpu.make_async_copy(up_from, up_ref, arrived.at[1]),
        pltpu.make_async_copy(down_from, down_ref, arrived.at[2]),
    ]
    total = blocks * PARTS
    size = blocks * count // total
    groups = size // TILE

    def part(ref, number):
        return ref.at[pl.ds(number * size, size)]

    def load_copy(number):
        return pltpu.make_async_copy(part(got_from, number), part(got, number), came.at[number])

    def store_copy(number):
        return pltpu.make_async_copy(part(back, number), part(back_to, number), gone.at[number])

    load_copy(0).start()
    for copy in weights[:2]:
        copy.start()
    for number in range(1, total):
        load_copy(number).start()
    weights[2].start()
    one = (((1,), (0,)), ((), ()))
    other = (((1,), (1,)), ((), ()))

    def dot(a, b, dims):
        return lax.dot_general(a, b, dims, preferred_element_type=jnp.float32)

    for block in range(blocks):
        for number in range(block * PARTS, (block + 1) * PARTS):
            load_copy(number).wait()
            for group in range(groups):
                at = number * size + group * TILE
                tiles = got[at : at + TILE]
                both = jnp.concatenate(
                    [tiles[:, 0].reshape(256, LANES), tiles[:, 1].reshape(256, LANES)], axis=1
                )
                both = swap(perm, both)
                to = slice(at - block * count, at - block * count + TILE)
                rows[block, to, :] = rows_from_stack(both[:, :LANES])
                cots[block, to, :] = rows_from_stack(both[:, LANES:])
        if block == 0:
            weights[0].wait()
            weights[1].wait()
        pre_gate = dot(rows[block], gate_ref[...], one)
        pre_up = dot(rows[block], up_ref[...], one)
        sig = 1.0 / (1.0 + jnp.exp(-pre_gate))
        silu = pre_gate * sig
        hidden = (silu * pre_up).astype(jnp.bfloat16)
        if block == 0:
            weights[2].wait()
        outs[block] = dot(hidden, down_ref[...], one).astype(jnp.bfloat16)
        hidden_grad = dot(cots[block], down_ref[...], other)
        gate_part = hidden_grad * pre_up * (sig * (1.0 + pre_gate * (1.0 - sig)))
        gate_part = gate_part.astype(jnp.bfloat16)
        up_part = (hidden_grad * silu).astype(jnp.bfloat16)
        grads[block] = (
            dot(gate_part, gate_ref[...], other) + dot(up_part, up_ref[...], other)
        ).astype(jnp.bfloat16)
        for number in range(block * PARTS, (block + 1) * PARTS):
            for group in range(groups):
                at = number * size + group * TILE
                to = slice(at - block * count, at - block * count + TILE)
                both = jnp.concatenate(
                    [columns_stacked(outs[block, to, :]), columns_stacked(grads[block, to, :])],
                    axis=1,
                )
                both = swap(perm, both)
                back[at : at + TILE, 0] = both[:, :LANES].reshape(TILE, TILE, LANES)
                back[at : at + TILE, 1] = both[:, LANES:].reshape(TILE, TILE, LANES)
            store_copy(number).start()
    for number in range(total):
        store_copy(number).wait()


def expert(got, gate, up, down):
    blocks = 2
    count = got.shape[0] // blocks
    weights = [gate, up, down]
    return pl.pallas_call(
        expert_kernel,
        out_shape=jax.ShapeDtypeStruct(got.shape, jnp.bfloat16),
        in_specs=[pl.BlockSpec(memory_space=HBM)] * 4,
        out_specs=pl.BlockSpec(memory_space=HBM),
        scratch_shapes=[pltpu.VMEM(got.shape, jnp.bfloat16)] * 2
        + [pltpu.VMEM((blocks, count, gate.shape[0]), jnp.bfloat16)] * 4
        + [pltpu.VMEM(w.shape, jnp.bfloat16) for w in weights]
        + [pltpu.SemaphoreType.DMA((3,))]
        + [pltpu.SemaphoreType.DMA((blocks * PARTS,))] * 2,
        compiler_params=pltpu.CompilerParams(vmem_limit_bytes=50 << 20),
        cost_estimate=pl.CostEstimate(
            flops=512 * 2048 * 512 * 12, bytes_accessed=14 << 20, transcendentals=512 * 512
        ),
    )(got, *weights)


def combine_kernel(
    slot_ref, weight_ref, rows_from, cot_ref, shared_ref, shared_grad_ref, mixed_ref, grad_ref,
    gate_ref, outputs, grads, mixed_tiles, grad_tiles, partial, came
):
    copies = [
        pltpu.make_async_copy(rows_from.at[:, 0], outputs, came.at[0]),
        pltpu.make_async_copy(rows_from.at[:, 1], grads, came.at[1]),
    ]
    for copy in copies:
        copy.start()
    perm = swap_matrix()
    count = cot_ref.shape[0]

    def gather_output(token, carry):
        cot = cot_ref[token].astype(jnp.float32)
        mixed = shared_ref[token]
        for k in range(2):
            output = outputs[slot_ref[k * count + token]].astype(jnp.float32)
            mixed = mixed + weight_ref[k * count + token] * output
            partial[k, token] = jnp.sum((cot * output).reshape(2, 8, LANES), axis=0)
        mixed_tiles[token] = mixed.astype(jnp.bfloat16)
        return carry

    def gather_grad(token, carry):
        grad = shared_grad_ref[token]
        for k in range(2):
            grad = grad + grads[slot_ref[k * count + token]].astype(jnp.float32)
        grad_tiles[token] = grad.astype(jnp.bfloat16)
        return carry

    copies[0].wait()
    lax.fori_loop(0, count, gather_output, 0, unroll=4)
    copies[1].wait()
    lax.fori_loop(0, count, gather_grad, 0, unroll=4)
    for group in range(count // TILE):
        at = slice(group * TILE, (group + 1) * TILE)
        both = jnp.concatenate(
            [mixed_tiles[at].reshape(256, LANES), grad_tiles[at].reshape(256, LANES)], axis=1
        )
        both = swap(perm, both)
        mixed_ref[at, :] = rows_from_stack(both[:, :LANES])
        grad_ref[at, :] = rows_from_stack(both[:, LANES:])
    ones = jnp.ones((8, LANES), jnp.float32)
    for k in range(2):
        sums = lax.dot_general(
            ones,
            jnp.sum(partial[k], axis=1),
            (((1,), (1,)), ((), ())),
            precision=lax.Precision.HIGHEST,
            preferred_element_type=jnp.float32,
        )
        gate_ref[k : k + 1, :] = sums[:1]


def combine(slots, weights, rows, cot, shared, shared_grad):
    count = cot.shape[0]
    width = TILE * LANES
    return pl.pallas_call(
        combine_kernel,
        out_shape=[
            jax.ShapeDtypeStruct((count, width), jnp.bfloat16),
            jax.ShapeDtypeStruct((count, width), jnp.bfloat16),
            jax.ShapeDtypeStruct((2, count), jnp.float32),
        ],
        in_specs=[pl.BlockSpec(memory_space=SMEM)] * 2
        + [pl.BlockSpec(memory_space=HBM)]
        + [pl.BlockSpec(memory_space=VMEM)] * 3,
        out_specs=[pl.BlockSpec(memory_space=VMEM)] * 3,
        scratch_shapes=[
            pltpu.VMEM((rows.shape[0], TILE, LANES), jnp.bfloat16),
            pltpu.VMEM((rows.shape[0], TILE, LANES), jnp.bfloat16),
            pltpu.VMEM((count, TILE, LANES), jnp.bfloat16),
            pltpu.VMEM((count, TILE, LANES), jnp.bfloat16),
            pltpu.VMEM((2, count, 8, LANES), jnp.float32),
            pltpu.SemaphoreType.DMA((2,)),
        ],
        compiler_params=pltpu.CompilerParams(vmem_limit_bytes=32 << 20),
        cost_estimate=pl.CostEstimate(
            flops=8 * 2 * 256**3, bytes_accessed=8 << 20, transcendentals=0
        ),
    )(slots, weights, rows, cot, shared, shared_grad)


def route_slots(chosen, count):
    number = jnp.arange(chosen.shape[0], dtype=jnp.int32)
    written = 2 * (number % count) + number // count
    same = (chosen[:, None] == chosen[None, :]) & (written[None, :] > written[:, None])
    return chosen * 2 + jnp.sum(same.astype(jnp.int32), axis=1)


def shared_expert(tokens, grad_out, gate, up, down, switch_vector):
    def dot(a, b, spec):
        return jnp.einsum(spec, a, b, preferred_element_type=jnp.float32)

    switch = jax.nn.sigmoid(jnp.dot(tokens, switch_vector, preferred_element_type=jnp.float32))
    pre_gate = dot(tokens, gate, "td,df->tf")
    pre_up = dot(tokens, up, "td,df->tf")
    hidden = (jax.nn.silu(pre_gate) * pre_up).astype(jnp.bfloat16)
    shared = dot(hidden, down, "tf,fd->td")
    cot = grad_out.astype(jnp.float32)
    shared_cot = (switch[:, None] * cot).astype(jnp.bfloat16)
    hidden_grad = dot(shared_cot, down, "td,fd->tf")
    gate_part = (hidden_grad * pre_up * silu_grad(pre_gate)).astype(jnp.bfloat16)
    up_part = (hidden_grad * jax.nn.silu(pre_gate)).astype(jnp.bfloat16)
    input_grad = dot(gate_part, gate, "tf,df->td") + dot(up_part, up, "tf,df->td")
    switch_grad = switch * (1.0 - switch) * jnp.sum(cot * shared, axis=1)
    grad = input_grad + switch_grad[:, None] * switch_vector.astype(jnp.float32)[None, :]
    return switch[:, None] * shared, grad


def local(
    tokens,
    expert_ids,
    gate_weights,
    grad_out,
    expert_gate,
    expert_up,
    expert_down,
    shared_gate,
    shared_up,
    shared_down,
    shared_switch,
):
    devices = lax.axis_size("tp") * lax.axis_size("ep")
    count = tokens.shape[0]
    tiled = (count, TILE, LANES)
    chosen = expert_ids.T.reshape(-1)
    weights = gate_weights.T.reshape(-1)
    sent = pack(chosen, weights, tokens, grad_out, devices)

    def exchange(rows):
        return lax.all_to_all(
            rows.reshape(devices, -1, LANES), AXES, split_axis=0, concat_axis=0, tiled=True
        ).reshape(2 * devices, 2, TILE, LANES)

    got = exchange(sent)
    all_in = lax.all_gather(
        jnp.concatenate([shared_gate, shared_up], axis=0), "tp", axis=1, tiled=True
    )
    got, all_in, shared_down, routes = lax.optimization_barrier((got, all_in, shared_down, chosen))
    all_gate, all_up = jnp.split(all_in, 2, axis=0)
    all_down = lax.all_gather(shared_down, "tp", axis=0, tiled=True)
    back = exchange(expert(got, expert_gate[0], expert_up[0], expert_down[0]))
    shared, shared_grad = shared_expert(
        tokens, grad_out, all_gate, all_up, all_down, shared_switch
    )
    mixed, grad_tokens, gate_grad = combine(
        route_slots(routes, count),
        weights,
        back,
        grad_out.reshape(tiled),
        shared.reshape(tiled),
        shared_grad.reshape(tiled),
    )
    return (mixed, grad_tokens, gate_grad.T)


def solution(mesh):
    rows = P(AXES, None)
    experts = P(AXES, None, None)
    placed = (rows, rows, rows, rows, experts, experts, experts)
    placed += (P(None, "tp"), P(None, "tp"), P("tp", None), P())
    return jax.shard_map(
        local, mesh=mesh, in_specs=placed, out_specs=(rows, rows, rows), check_vma=False
    )
```

time: 279 us -> 261 us (0.935)
  waiting for transfers between devices: 195 us -> 184 us
  Pallas kernels: 26.6 us -> 21.9 us
    all_to_all x2, waiting for transfers between devices: 96.6 us -> 53.4 us  [exchange(): lax.all_to_all(rows.reshape(devices, -1, LANES), AXES, split_axis=0, conc...]
    all_gather x2 -> x1, waiting for transfers between devices: 53.3 us -> 83.2 us  [local(): lax.all_gather(jnp.concatenate([shared_gate, shared_up], axis=0), 'tp', a...]
    pallas_call x1, Pallas kernels: 19.5 us -> 13.4 us  [expert(): pl.pallas_call(expert_kernel, out_shape=jax.ShapeDtypeStruct(got.shape, j...]
    all_gather x1, waiting for transfers between devices: 43.4 us -> 46.3 us  [local(): all_down = lax.all_gather(shared_down, 'tp', axis=0, tiled=True)]
    unnamed x26 -> x36, local copies, waits for them, and re-layouts: 7.6 us -> 6.59 us
  transfers between devices with their start and end apart: 5 -> 4, of which waited for: 3 -> 4; matrix products, arithmetic and copies ran while one was open for 3% -> 4% of each run, Pallas kernels for 7% -> 0%
where the time goes in v3:
time: 261 us
  waiting for transfers between devices  184 us (70%)
  starting transfers between devices  24.7 us (9%)
  Pallas kernels  21.9 us (8%)
  between operations  14.3 us (5%)
  matrix products  8.34 us (3%)
  local copies, waits for them, and re-layouts  6.59 us (3%)
    all_gather x1, waiting for transfers between devices, local(): lax.all_gather(jnp.concatenate([shared_gate, shared_up], axis=0), 'tp', a...  83.2 us
    all_to_all x2, waiting for transfers between devices, exchange(): lax.all_to_all(rows.reshape(devices, -1, LANES), AXES, split_axis=0, conc...  53.4 us
    all_gather x1, waiting for transfers between devices, local(): all_down = lax.all_gather(shared_down, 'tp', axis=0, tiled=True)  46.3 us
    all_to_all x2, starting transfers between devices, exchange(): lax.all_to_all(rows.reshape(devices, -1, LANES), AXES, split_axis=0, conc...  24.6 us
    pallas_call x1, Pallas kernels, expert(): pl.pallas_call(expert_kernel, out_shape=jax.ShapeDtypeStruct(got.shape, j...  13.4 us
    dot_general x6, matrix products, dot(): return jnp.einsum(spec, a, b, preferred_element_type=jnp.float32)  8.1 us
    unnamed x36, local copies, waits for them, and re-layouts  6.59 us
  transfers between devices with their start and end apart: 4, of which 4 were waited for; matrix products, arithmetic and copies ran while one was open for 4% of the time, Pallas kernels for 0%

profile of v3, /device:TPU:1, one launch (start us, length us, event | category | flops | bytes accessed | tf_op | source)
XLA Modules:
  0.0 260.8 jit_solution(6559422939915175335)
XLA Ops:
  7.2 1.0 copy-done.1
  8.2 1.0 copy-done.3
  9.3 0.7 copy-done.5
  9.9 0.7 copy-done.7
  10.6 3.7 %shard_map.130 = bf16[256,2,2,16,128]{4,3,2,1,0:T(8,128)(2,1)S(1)} custom-call(s32[256]{0:T(256)S(1)} %bitcast.47, f32[256]{0:T(256)S(1)} %bitcast.50, bf16[128,2048]{1,0:T(8,128)(2,1)S(1)} %copy-done.3, bf16[128,2048]{1,0:T(8,128)(2,1)S(1)} %copy-done.1), custom_call_target="tpu_custom_call" | custom-call | flops 268435456 | bytes 5242880 | tf_op jit(solution)/shard_map/pallas_call | solution.py:101
  14.3 2.0 copy-done
  16.3 16.7 %all-to-all-start = ((bf16[256,64,128]{2,1,0:T(8,128)(2,1)}), bf16[256,64,128]{2,1,0:T(8,128)(2,1)}, u32[]{:S(2)}, u32[]{:S(2)}) async-start(bf16[256,64,128]{2,1,0:T(8,128)(2,1)} %bitcast.42), calls=%async_computation | async-start | bytes 8388608 | tf_op jit(solution)/shard_map/all_to_all | solution.py:352
  32.9 0.0 all-gather.3.cloned.1.call-start
  33.0 1.1 pad_maximum_fusion
  34.1 0.0 all-gather.3.cloned.1.call-update
  34.1 83.2 %all-gather.3.cloned.1.call-done = bf16[4096,512]{1,0:T(8,128)(2,1)} async-done(((bf16[4096,128]{1,0:T(8,128)(2,1)}), bf16[4096,512]{1,0:T(8,128)(2,1)}) %all-gather.3.cloned.1.call-update) | async-done | bytes 4194320 | tf_op jit(solution)/shard_map/all_gather | solution.py:357
  117.3 13.0 %all-to-all-done = bf16[256,64,128]{2,1,0:T(8,128)(2,1)} async-done(((bf16[256,64,128]{2,1,0:T(8,128)(2,1)}), bf16[256,64,128]{2,1,0:T(8,128)(2,1)}, u32[]{:S(2)}, u32[]{:S(2)}) %all-to-all-start) | async-done | bytes 4194336 | tf_op jit(solution)/shard_map/all_to_all | solution.py:352
  130.3 13.4 %shard_map.131 = bf16[512,2,16,128]{3,2,1,0:T(8,128)(2,1)} custom-call(bf16[512,2,16,128]{3,2,1,0:T(8,128)(2,1)} %bitcast.5.got_from, bf16[2048,512]{1,0:T(8,128)(2,1)S(1)} %bitcast.52, bf16[2048,512]{1,0:T(8,128)(2,1)} %bitcast.54, bf16[512,2048]{1,0:T(8,128)(2,1)} %bitcast.55), custom_call_target="tpu_custom_call" | custom-call | flops 6442450944 | bytes 14680064 | tf_op jit(solution)/shard_map/pallas_call | solution.py:204
  143.7 8.0 %all-to-all-start.1 = ((bf16[256,64,128]{2,1,0:T(8,128)(2,1)}), bf16[256,64,128]{2,1,0:T(8,128)(2,1)}, u32[]{:S(2)}, u32[]{:S(2)}) async-start(bf16[256,64,128]{2,1,0:T(8,128)(2,1)} %bitcast.53), calls=%async_computation.1 | async-start | bytes 8388608 | tf_op jit(solution)/shard_map/all_to_all | solution.py:352
  151.7 0.0 all-gather.5.cloned.1.call-start
  151.8 0.7 all-gather.5.cloned.1.call-update
  152.5 0.1 copy.19
  152.7 0.2 fusion.20
  152.9 0.2 convert_reduce_fusion
  153.2 2.5 fusion.11
  155.6 0.3 copy-done.11
  156.0 0.7 fusion.14
  156.7 46.3 %all-gather.5.cloned.1.call-done = bf16[512,2048]{1,0:T(8,128)(2,1)} async-done(((bf16[128,2048]{1,0:T(8,128)(2,1)}), bf16[512,2048]{1,0:T(8,128)(2,1)}) %all-gather.5.cloned.1.call-update) | async-done | bytes 2097168 | tf_op jit(solution)/shard_map/all_gather | solution.py:362
  203.1 2.3 fusion.22
  205.4 0.8 fusion.23
  206.2 0.3 copy-done.12
  206.5 0.9 fusion.4
  207.4 0.9 fusion.8
  208.3 0.2 copy.21
  208.5 0.2 copy.20
  208.7 40.4 %all-to-all-done.1 = bf16[256,64,128]{2,1,0:T(8,128)(2,1)} async-done(((bf16[256,64,128]{2,1,0:T(8,128)(2,1)}), bf16[256,64,128]{2,1,0:T(8,128)(2,1)}, u32[]{:S(2)}, u32[]{:S(2)}) %all-to-all-start.1) | async-done | bytes 4194336 | tf_op jit(solution)/shard_map/all_to_all | solution.py:352
  249.1 4.8 %shard_map.132 = (bf16[128,2048]{1,0:T(8,128)(2,1)}, bf16[128,2048]{1,0:T(8,128)(2,1)}, f32[2,128]{1,0:T(2,128)}) custom-call(s32[256]{0:T(256)S(1)} %multiply_add_fusion.slot_ref, f32[256]{0:T(256)S(1)} %bitcast.51, bf16[512,2,16,128]{3,2,1,0:T(8,128)(2,1)} %bitcast.10.rows_from, bf16[128,16,128]{2,1,0:T(8,128)(2,1)S(1)} %bitcast.46, ...), custom_call_target="tpu_custom_call" | custom-call | flops 268435456 | bytes 8388608 | tf_op jit(solution)/shard_map/pallas_call | solution.py:278
  (30 shorter events, 0.1 us)
Async XLA Ops:
  7.2 1.0 copy-start.1
  8.2 1.0 copy-start.3
  9.3 0.7 copy-start.5
  9.9 0.7 copy-start.7
  14.3 2.0 copy-start
  16.3 16.7 %copy-start.13 = (bf16[2048,128]{1,0:T(8,128)(2,1)S(1)}, bf16[2048,128]{1,0:T(8,128)(2,1)}, u32[]{:S(2)}) copy-start(bf16[2048,128]{1,0:T(8,128)(2,1)} %param.19) | copy-start | bytes 1572868
  16.3 16.7 %copy-start.14 = (bf16[2048,128]{1,0:T(8,128)(2,1)S(1)}, bf16[2048,128]{1,0:T(8,128)(2,1)}, u32[]{:S(2)}) copy-start(bf16[2048,128]{1,0:T(8,128)(2,1)} %param.18) | copy-start | bytes 1572868
  16.3 114.0 %all-to-all-start = ((bf16[256,64,128]{2,1,0:T(8,128)(2,1)}), bf16[256,64,128]{2,1,0:T(8,128)(2,1)}, u32[]{:S(2)}, u32[]{:S(2)}) async-start(bf16[256,64,128]{2,1,0:T(8,128)(2,1)} %bitcast.42), calls=%async_computation | async-start | bytes 8388608 | tf_op jit(solution)/shard_map/all_to_all | solution.py:352
  32.9 97.4 %copy-start.9 = (bf16[1,2048,512]{2,1,0:T(8,128)(2,1)S(1)}, bf16[1,2048,512]{2,1,0:T(8,128)(2,1)}, u32[]{:S(2)}) copy-start(bf16[1,2048,512]{2,1,0:T(8,128)(2,1)} %param.15) | copy-start | bytes 6291460
  32.9 84.4 %all-gather.3.cloned.1.call-start = ((), (), s32[]{:S(2)}) async-start(), calls=%async_computation.2 | async-start | bytes 5242880 | tf_op jit(solution)/shard_map/all_gather | solution.py:357
  143.7 8.8 %copy-start.15 = (bf16[2048]{0:T(1024)(128)(2,1)S(1)}, bf16[2048]{0:T(1024)(128)(2,1)}, u32[]{:S(2)}) copy-start(bf16[2048]{0:T(1024)(128)(2,1)} %param.21) | copy-start | bytes 12292
  143.7 8.8 %copy-start.2 = (bf16[128,2048]{1,0:T(8,128)(2,1)S(1)}, bf16[128,2048]{1,0:T(8,128)(2,1)}, u32[]{:S(2)}) copy-start(bf16[128,2048]{1,0:T(8,128)(2,1)} %cot_from.1) | copy-start | bytes 1572868
  143.7 8.9 %copy-start.4 = (bf16[128,2048]{1,0:T(8,128)(2,1)S(1)}, bf16[128,2048]{1,0:T(8,128)(2,1)}, u32[]{:S(2)}) copy-start(bf16[128,2048]{1,0:T(8,128)(2,1)} %tokens_from.1) | copy-start | bytes 1572868
  143.7 105.4 %all-to-all-start.1 = ((bf16[256,64,128]{2,1,0:T(8,128)(2,1)}), bf16[256,64,128]{2,1,0:T(8,128)(2,1)}, u32[]{:S(2)}, u32[]{:S(2)}) async-start(bf16[256,64,128]{2,1,0:T(8,128)(2,1)} %bitcast.53), calls=%async_computation.1 | async-start | bytes 8388608 | tf_op jit(solution)/shard_map/all_to_all | solution.py:352
  151.7 1.2 copy-start.6
  151.7 51.3 %all-gather.5.cloned.1.call-start = ((), (), s32[]{:S(2)}) async-start(), calls=%async_computation.3 | async-start | bytes 2621440 | tf_op jit(solution)/shard_map/all_gather | solution.py:362
  153.2 2.8 %copy-start.11 = (bf16[4096,512]{1,0:T(8,128)(2,1)S(1)}, bf16[4096,512]{1,0:T(8,128)(2,1)}, u32[]{:S(2)}) copy-start(bf16[4096,512]{1,0:T(8,128)(2,1)} %all-gather.3.cloned.1.call-done) | copy-start | bytes 12582916
  203.1 2.3 copy-start.10
  203.1 3.5 %copy-start.12 = (bf16[4096,512]{1,0:T(8,128)(2,1)S(1)}, bf16[4096,512]{1,0:T(8,128)(2,1)}, u32[]{:S(2)}) copy-start(bf16[4096,512]{1,0:T(8,128)(2,1)} %all-gather.3.cloned.1.call-done) | copy-start | bytes 12582916
  208.3 40.8 %copy-start.8 = (f32[128,2]{0,1:T(2,128)S(1)}, f32[128,2]{0,1:T(2,128)}, u32[]{:S(2)}) copy-start(f32[128,2]{0,1:T(2,128)} %param.13) | copy-start | bytes 3076
Sparse Core Ops, SparseCore 0:
  35.6 81.7 all-gather.2
  154.4 48.6 all-gather.4

commit v4 on v3

--- a/solution.py
+++ b/solution.py
@@ -107,7 +107,7 @@
         + [pltpu.VMEM((count, TILE, LANES), jnp.bfloat16)] * 2
         + [pltpu.VMEM((experts, 2, TILE, LANES), jnp.bfloat16)] * 2
         + [pltpu.SemaphoreType.DMA((4,))],
-        compiler_params=pltpu.CompilerParams(vmem_limit_bytes=32 << 20),
+        compiler_params=pltpu.CompilerParams(vmem_limit_bytes=60 << 20),
         cost_estimate=pl.CostEstimate(
             flops=8 * 2 * 256**3, bytes_accessed=5 << 20, transcendentals=0
         ),

time: 261 us -> 257 us (0.985)
  local copies, waits for them, and re-layouts: 6.59 us -> 1.18 us
    unnamed x36 -> x26, local copies, waits for them, and re-layouts: 6.59 us -> 1.18 us
where the time goes in v4:
time: 257 us
  waiting for transfers between devices  184 us (72%)
  starting transfers between devices  24.7 us (10%)
  Pallas kernels  23.3 us (9%)
  between operations  14.3 us (6%)
  matrix products  8.33 us (3%)
    all_gather x1, waiting for transfers between devices, local(): lax.all_gather(jnp.concatenate([shared_gate, shared_up], axis=0), 'tp', a...  83.2 us
    all_to_all x2, waiting for transfers between devices, exchange(): lax.all_to_all(rows.reshape(devices, -1, LANES), AXES, split_axis=0, conc...  53.4 us
    all_gather x1, waiting for transfers between devices, local(): all_down = lax.all_gather(shared_down, 'tp', axis=0, tiled=True)  46.3 us
    all_to_all x2, starting transfers between devices, exchange(): lax.all_to_all(rows.reshape(devices, -1, LANES), AXES, split_axis=0, conc...  24.6 us
    pallas_call x1, Pallas kernels, expert(): pl.pallas_call(expert_kernel, out_shape=jax.ShapeDtypeStruct(got.shape, j...  13.4 us
    dot_general x6, matrix products, dot(): return jnp.einsum(spec, a, b, preferred_element_type=jnp.float32)  8.09 us
  transfers between devices with their start and end apart: 4, of which 4 were waited for; matrix products, arithmetic and copies ran while one was open for 4% of the time, Pallas kernels for 0%

profile of v4, /device:TPU:1, one launch (start us, length us, event | category | flops | bytes accessed | tf_op | source)
XLA Modules:
  0.0 256.8 jit_solution(2285995194459733481)
XLA Ops:
  7.2 5.1 %shard_map.130 = bf16[256,2,2,16,128]{4,3,2,1,0:T(8,128)(2,1)} custom-call(s32[256]{0:T(256)} %bitcast.51, f32[256]{0:T(256)} %bitcast.45, bf16[128,2048]{1,0:T(8,128)(2,1)} %tokens_from.1, bf16[128,2048]{1,0:T(8,128)(2,1)} %cot_from.1), custom_call_target="tpu_custom_call" | custom-call | flops 268435456 | bytes 5242880 | tf_op jit(solution)/shard_map/pallas_call | solution.py:101
  12.2 0.0 copy-start.7
  12.2 0.0 copy-start.8
  12.3 16.7 %all-to-all-start = ((bf16[256,64,128]{2,1,0:T(8,128)(2,1)}), bf16[256,64,128]{2,1,0:T(8,128)(2,1)}, u32[]{:S(2)}, u32[]{:S(2)}) async-start(bf16[256,64,128]{2,1,0:T(8,128)(2,1)} %bitcast.48), calls=%async_computation | async-start | bytes 8388608 | tf_op jit(solution)/shard_map/all_to_all | solution.py:352
  28.9 0.0 copy-start.1
  28.9 0.0 all-gather.3.cloned.1.call-start
  29.0 1.1 pad_maximum_fusion
  30.1 0.0 all-gather.3.cloned.1.call-update
  30.1 83.2 %all-gather.3.cloned.1.call-done = bf16[4096,512]{1,0:T(8,128)(2,1)} async-done(((bf16[4096,128]{1,0:T(8,128)(2,1)}), bf16[4096,512]{1,0:T(8,128)(2,1)}) %all-gather.3.cloned.1.call-update) | async-done | bytes 4194320 | tf_op jit(solution)/shard_map/all_gather | solution.py:357
  113.3 13.0 %all-to-all-done = bf16[256,64,128]{2,1,0:T(8,128)(2,1)} async-done(((bf16[256,64,128]{2,1,0:T(8,128)(2,1)}), bf16[256,64,128]{2,1,0:T(8,128)(2,1)}, u32[]{:S(2)}, u32[]{:S(2)}) %all-to-all-start) | async-done | bytes 4194336 | tf_op jit(solution)/shard_map/all_to_all | solution.py:352
  126.3 13.4 %shard_map.131 = bf16[512,2,16,128]{3,2,1,0:T(8,128)(2,1)} custom-call(bf16[512,2,16,128]{3,2,1,0:T(8,128)(2,1)} %bitcast.5.got_from, bf16[2048,512]{1,0:T(8,128)(2,1)S(1)} %bitcast.47, bf16[2048,512]{1,0:T(8,128)(2,1)} %bitcast.54, bf16[512,2048]{1,0:T(8,128)(2,1)} %bitcast.55), custom_call_target="tpu_custom_call" | custom-call | flops 6442450944 | bytes 14680064 | tf_op jit(solution)/shard_map/pallas_call | solution.py:204
  139.7 0.0 copy-start.3
  139.7 0.0 copy-start.4
  139.7 8.0 %all-to-all-start.1 = ((bf16[256,64,128]{2,1,0:T(8,128)(2,1)}), bf16[256,64,128]{2,1,0:T(8,128)(2,1)}, u32[]{:S(2)}, u32[]{:S(2)}) async-start(bf16[256,64,128]{2,1,0:T(8,128)(2,1)} %bitcast.50), calls=%async_computation.1 | async-start | bytes 8388608 | tf_op jit(solution)/shard_map/all_to_all | solution.py:352
  147.7 0.0 all-gather.5.cloned.1.call-start
  147.8 0.7 all-gather.5.cloned.1.call-update
  148.5 0.1 copy.19
  148.7 0.2 fusion.20
  148.9 0.2 convert_reduce_fusion
  149.2 2.5 fusion.11
  151.7 0.3 copy-done.5
  152.0 0.8 fusion.14
  152.7 46.3 %all-gather.5.cloned.1.call-done = bf16[512,2048]{1,0:T(8,128)(2,1)} async-done(((bf16[128,2048]{1,0:T(8,128)(2,1)}), bf16[512,2048]{1,0:T(8,128)(2,1)}) %all-gather.5.cloned.1.call-update) | async-done | bytes 2097168 | tf_op jit(solution)/shard_map/all_gather | solution.py:362
  199.1 2.3 fusion.22
  201.4 0.8 fusion.23
  202.2 0.3 copy-done.6
  202.5 0.8 fusion.4
  203.4 0.9 fusion.8
  204.3 0.2 copy.21
  204.5 0.2 copy.20
  204.7 40.4 %all-to-all-done.1 = bf16[256,64,128]{2,1,0:T(8,128)(2,1)} async-done(((bf16[256,64,128]{2,1,0:T(8,128)(2,1)}), bf16[256,64,128]{2,1,0:T(8,128)(2,1)}, u32[]{:S(2)}, u32[]{:S(2)}) %all-to-all-start.1) | async-done | bytes 4194336 | tf_op jit(solution)/shard_map/all_to_all | solution.py:352
  245.1 4.8 %shard_map.132 = (bf16[128,2048]{1,0:T(8,128)(2,1)}, bf16[128,2048]{1,0:T(8,128)(2,1)}, f32[2,128]{1,0:T(2,128)}) custom-call(s32[256]{0:T(256)S(1)} %multiply_add_fusion.slot_ref, f32[256]{0:T(256)S(1)} %bitcast.46, bf16[512,2,16,128]{3,2,1,0:T(8,128)(2,1)} %bitcast.10.rows_from, bf16[128,16,128]{2,1,0:T(8,128)(2,1)S(1)} %bitcast.44, ...), custom_call_target="tpu_custom_call" | custom-call | flops 268435456 | bytes 8388608 | tf_op jit(solution)/shard_map/pallas_call | solution.py:278
  (20 shorter events, 0.1 us)
Async XLA Ops:
  12.2 16.8 %copy-start.7 = (bf16[2048,128]{1,0:T(8,128)(2,1)S(1)}, bf16[2048,128]{1,0:T(8,128)(2,1)}, u32[]{:S(2)}) copy-start(bf16[2048,128]{1,0:T(8,128)(2,1)} %param.19) | copy-start | bytes 1572868
  12.2 16.8 %copy-start.8 = (bf16[2048,128]{1,0:T(8,128)(2,1)S(1)}, bf16[2048,128]{1,0:T(8,128)(2,1)}, u32[]{:S(2)}) copy-start(bf16[2048,128]{1,0:T(8,128)(2,1)} %param.18) | copy-start | bytes 1572868
  12.3 114.0 %all-to-all-start = ((bf16[256,64,128]{2,1,0:T(8,128)(2,1)}), bf16[256,64,128]{2,1,0:T(8,128)(2,1)}, u32[]{:S(2)}, u32[]{:S(2)}) async-start(bf16[256,64,128]{2,1,0:T(8,128)(2,1)} %bitcast.48), calls=%async_computation | async-start | bytes 8388608 | tf_op jit(solution)/shard_map/all_to_all | solution.py:352
  28.9 97.4 %copy-start.1 = (bf16[1,2048,512]{2,1,0:T(8,128)(2,1)S(1)}, bf16[1,2048,512]{2,1,0:T(8,128)(2,1)}, u32[]{:S(2)}) copy-start(bf16[1,2048,512]{2,1,0:T(8,128)(2,1)} %param.15) | copy-start | bytes 6291460
  28.9 84.4 %all-gather.3.cloned.1.call-start = ((), (), s32[]{:S(2)}) async-start(), calls=%async_computation.2 | async-start | bytes 5242880 | tf_op jit(solution)/shard_map/all_gather | solution.py:357
  139.7 8.8 %copy-start.10 = (bf16[2048]{0:T(1024)(128)(2,1)S(1)}, bf16[2048]{0:T(1024)(128)(2,1)}, u32[]{:S(2)}) copy-start(bf16[2048]{0:T(1024)(128)(2,1)} %param.21) | copy-start | bytes 12292
  139.7 8.8 %copy-start.3 = (bf16[128,2048]{1,0:T(8,128)(2,1)S(1)}, bf16[128,2048]{1,0:T(8,128)(2,1)}, u32[]{:S(2)}) copy-start(bf16[128,2048]{1,0:T(8,128)(2,1)} %cot_from.1) | copy-start | bytes 1572868
  139.7 8.9 %copy-start.4 = (bf16[128,2048]{1,0:T(8,128)(2,1)S(1)}, bf16[128,2048]{1,0:T(8,128)(2,1)}, u32[]{:S(2)}) copy-start(bf16[128,2048]{1,0:T(8,128)(2,1)} %tokens_from.1) | copy-start | bytes 1572868
  139.7 105.4 %all-to-all-start.1 = ((bf16[256,64,128]{2,1,0:T(8,128)(2,1)}), bf16[256,64,128]{2,1,0:T(8,128)(2,1)}, u32[]{:S(2)}, u32[]{:S(2)}) async-start(bf16[256,64,128]{2,1,0:T(8,128)(2,1)} %bitcast.50), calls=%async_computation.1 | async-start | bytes 8388608 | tf_op jit(solution)/shard_map/all_to_all | solution.py:352
  147.7 1.2 copy-start.9
  147.7 51.3 %all-gather.5.cloned.1.call-start = ((), (), s32[]{:S(2)}) async-start(), calls=%async_computation.3 | async-start | bytes 2621440 | tf_op jit(solution)/shard_map/all_gather | solution.py:362
  149.1 2.8 %copy-start.5 = (bf16[4096,512]{1,0:T(8,128)(2,1)S(1)}, bf16[4096,512]{1,0:T(8,128)(2,1)}, u32[]{:S(2)}) copy-start(bf16[4096,512]{1,0:T(8,128)(2,1)} %all-gather.3.cloned.1.call-done) | copy-start | bytes 12582916
  199.1 2.3 copy-start.2
  199.1 3.5 %copy-start.6 = (bf16[4096,512]{1,0:T(8,128)(2,1)S(1)}, bf16[4096,512]{1,0:T(8,128)(2,1)}, u32[]{:S(2)}) copy-start(bf16[4096,512]{1,0:T(8,128)(2,1)} %all-gather.3.cloned.1.call-done) | copy-start | bytes 12582916
  204.3 40.8 %copy-start = (f32[128,2]{0,1:T(2,128)S(1)}, f32[128,2]{0,1:T(2,128)}, u32[]{:S(2)}) copy-start(f32[128,2]{0,1:T(2,128)} %param.13) | copy-start | bytes 3076
Sparse Core Ops, SparseCore 0:
  31.6 81.7 all-gather.2
  150.4 48.6 all-gather.4

commit v5 on v4

--- a/solution.py
+++ b/solution.py
@@ -138,12 +138,12 @@
     def store_copy(number):
         return pltpu.make_async_copy(part(back, number), part(back_to, number), gone.at[number])
 
-    load_copy(0).start()
-    for copy in weights[:2]:
+    for number in range(PARTS):
+        load_copy(number).start()
+    for copy in weights:
         copy.start()
-    for number in range(1, total):
+    for number in range(PARTS, total):
         load_copy(number).start()
-    weights[2].start()
     one = (((1,), (0,)), ((), ()))
     other = (((1,), (1,)), ((), ()))
 
@@ -198,7 +198,7 @@
 
 
 def expert(got, gate, up, down):
-    blocks = 2
+    blocks = 1
     count = got.shape[0] // blocks
     weights = [gate, up, down]
     return pl.pallas_call(
@@ -226,8 +226,7 @@
         pltpu.make_async_copy(rows_from.at[:, 0], outputs, came.at[0]),
         pltpu.make_async_copy(rows_from.at[:, 1], grads, came.at[1]),
     ]
-    for copy in copies:
-        copy.start()
+    copies[0].start()
     perm = swap_matrix()
     count = cot_ref.shape[0]
 
@@ -249,9 +248,10 @@
         return carry
 
     copies[0].wait()
-    lax.fori_loop(0, count, gather_output, 0, unroll=4)
+    copies[1].start()
+    lax.fori_loop(0, count, gather_output, 0, unroll=16)
     copies[1].wait()
-    lax.fori_loop(0, count, gather_grad, 0, unroll=4)
+    lax.fori_loop(0, count, gather_grad, 0, unroll=16)
     for group in range(count // TILE):
         at = slice(group * TILE, (group + 1) * TILE)
         both = jnp.concatenate(

time: 257 us -> 257 us (level)
  no operation moved by 1% of the time
where the time goes in v5:
time: 257 us; the launch traced here: 256 us
  waiting for transfers between devices  183 us (71%)
  starting transfers between devices  24.7 us (10%)
  Pallas kernels  23 us (9%)
  between operations  14.3 us (6%)
  matrix products  8.33 us (3%)
    all_gather x1, waiting for transfers between devices, local(): lax.all_gather(jnp.concatenate([shared_gate, shared_up], axis=0), 'tp', a...  83.2 us
    all_to_all x2, waiting for transfers between devices, exchange(): lax.all_to_all(rows.reshape(devices, -1, LANES), AXES, split_axis=0, conc...  53.4 us
    all_gather x1, waiting for transfers between devices, local(): all_down = lax.all_gather(shared_down, 'tp', axis=0, tiled=True)  46.3 us
    all_to_all x2, starting transfers between devices, exchange(): lax.all_to_all(rows.reshape(devices, -1, LANES), AXES, split_axis=0, conc...  24.5 us
    pallas_call x1, Pallas kernels, expert(): pl.pallas_call(expert_kernel, out_shape=jax.ShapeDtypeStruct(got.shape, j...  12.4 us
    dot_general x6, matrix products, dot(): return jnp.einsum(spec, a, b, preferred_element_type=jnp.float32)  8.09 us
    pallas_call x1, Pallas kernels, combine(): pl.pallas_call(combine_kernel, out_shape=[jax.ShapeDtypeStruct((count, wi...  5.59 us
  transfers between devices with their start and end apart: 4, of which 4 were waited for; matrix products, arithmetic and copies ran while one was open for 4% of the time, Pallas kernels for 0%

profile of v5, /device:TPU:1, one launch (start us, length us, event | category | flops | bytes accessed | tf_op | source)
XLA Modules:
  0.0 256.4 jit_solution(13980947758587468116)
XLA Ops:
  7.2 5.1 %shard_map.130 = bf16[256,2,2,16,128]{4,3,2,1,0:T(8,128)(2,1)} custom-call(s32[256]{0:T(256)} %bitcast.51, f32[256]{0:T(256)} %bitcast.45, bf16[128,2048]{1,0:T(8,128)(2,1)} %tokens_from.1, bf16[128,2048]{1,0:T(8,128)(2,1)} %cot_from.1), custom_call_target="tpu_custom_call" | custom-call | flops 268435456 | bytes 5242880 | tf_op jit(solution)/shard_map/pallas_call | solution.py:101
  12.2 0.0 copy-start.7
  12.2 0.0 copy-start.8
  12.3 16.7 %all-to-all-start = ((bf16[256,64,128]{2,1,0:T(8,128)(2,1)}), bf16[256,64,128]{2,1,0:T(8,128)(2,1)}, u32[]{:S(2)}, u32[]{:S(2)}) async-start(bf16[256,64,128]{2,1,0:T(8,128)(2,1)} %bitcast.48), calls=%async_computation | async-start | bytes 8388608 | tf_op jit(solution)/shard_map/all_to_all | solution.py:352
  28.9 0.0 all-gather.3.cloned.1.call-start
  29.0 1.1 pad_maximum_fusion
  30.1 0.0 all-gather.3.cloned.1.call-update
  30.1 83.2 %all-gather.3.cloned.1.call-done = bf16[4096,512]{1,0:T(8,128)(2,1)} async-done(((bf16[4096,128]{1,0:T(8,128)(2,1)}), bf16[4096,512]{1,0:T(8,128)(2,1)}) %all-gather.3.cloned.1.call-update) | async-done | bytes 4194320 | tf_op jit(solution)/shard_map/all_gather | solution.py:357
  113.3 13.0 %all-to-all-done = bf16[256,64,128]{2,1,0:T(8,128)(2,1)} async-done(((bf16[256,64,128]{2,1,0:T(8,128)(2,1)}), bf16[256,64,128]{2,1,0:T(8,128)(2,1)}, u32[]{:S(2)}, u32[]{:S(2)}) %all-to-all-start) | async-done | bytes 4194336 | tf_op jit(solution)/shard_map/all_to_all | solution.py:352
  126.3 12.4 %shard_map.131 = bf16[512,2,16,128]{3,2,1,0:T(8,128)(2,1)} custom-call(bf16[512,2,16,128]{3,2,1,0:T(8,128)(2,1)} %bitcast.5.got_from, bf16[2048,512]{1,0:T(8,128)(2,1)S(1)} %bitcast.47, bf16[2048,512]{1,0:T(8,128)(2,1)} %bitcast.54, bf16[512,2048]{1,0:T(8,128)(2,1)} %bitcast.55), custom_call_target="tpu_custom_call" | custom-call | flops 6442450944 | bytes 14680064 | tf_op jit(solution)/shard_map/pallas_call | solution.py:204
  138.7 0.0 copy-start.10
  138.7 0.0 copy-start.3
  138.7 7.8 %all-to-all-start.1 = ((bf16[256,64,128]{2,1,0:T(8,128)(2,1)}), bf16[256,64,128]{2,1,0:T(8,128)(2,1)}, u32[]{:S(2)}, u32[]{:S(2)}) async-start(bf16[256,64,128]{2,1,0:T(8,128)(2,1)} %bitcast.50), calls=%async_computation.1 | async-start | bytes 8388608 | tf_op jit(solution)/shard_map/all_to_all | solution.py:352
  146.5 0.0 copy-start.9
  146.5 0.2 all-gather.5.cloned.1.call-start
  146.8 0.5 all-gather.5.cloned.1.call-update
  147.3 0.1 copy.19
  147.5 0.2 fusion.20
  147.7 0.2 convert_reduce_fusion
  148.0 2.5 fusion.11
  150.5 0.3 copy-done.5
  150.8 0.7 fusion.14
  151.5 46.3 %all-gather.5.cloned.1.call-done = bf16[512,2048]{1,0:T(8,128)(2,1)} async-done(((bf16[128,2048]{1,0:T(8,128)(2,1)}), bf16[512,2048]{1,0:T(8,128)(2,1)}) %all-gather.5.cloned.1.call-update) | async-done | bytes 2097168 | tf_op jit(solution)/shard_map/all_gather | solution.py:362
  197.9 2.3 fusion.22
  200.2 0.8 fusion.23
  201.0 0.3 copy-done.6
  201.3 0.8 fusion.4
  202.2 0.9 fusion.8
  203.1 0.2 copy.21
  203.3 0.2 copy.20
  203.5 40.4 %all-to-all-done.1 = bf16[256,64,128]{2,1,0:T(8,128)(2,1)} async-done(((bf16[256,64,128]{2,1,0:T(8,128)(2,1)}), bf16[256,64,128]{2,1,0:T(8,128)(2,1)}, u32[]{:S(2)}, u32[]{:S(2)}) %all-to-all-start.1) | async-done | bytes 4194336 | tf_op jit(solution)/shard_map/all_to_all | solution.py:352
  243.9 5.6 %shard_map.132 = (bf16[128,2048]{1,0:T(8,128)(2,1)}, bf16[128,2048]{1,0:T(8,128)(2,1)}, f32[2,128]{1,0:T(2,128)}) custom-call(s32[256]{0:T(256)S(1)} %multiply_add_fusion.slot_ref, f32[256]{0:T(256)S(1)} %bitcast.46, bf16[512,2,16,128]{3,2,1,0:T(8,128)(2,1)} %bitcast.10.rows_from, bf16[128,16,128]{2,1,0:T(8,128)(2,1)S(1)} %bitcast.44, ...), custom_call_target="tpu_custom_call" | custom-call | flops 268435456 | bytes 8388608 | tf_op jit(solution)/shard_map/pallas_call | solution.py:278
  (20 shorter events, 0.1 us)
Async XLA Ops:
  12.2 16.8 %copy-start.7 = (bf16[2048,128]{1,0:T(8,128)(2,1)S(1)}, bf16[2048,128]{1,0:T(8,128)(2,1)}, u32[]{:S(2)}) copy-start(bf16[2048,128]{1,0:T(8,128)(2,1)} %param.19) | copy-start | bytes 1572868
  12.2 16.8 %copy-start.8 = (bf16[2048,128]{1,0:T(8,128)(2,1)S(1)}, bf16[2048,128]{1,0:T(8,128)(2,1)}, u32[]{:S(2)}) copy-start(bf16[2048,128]{1,0:T(8,128)(2,1)} %param.18) | copy-start | bytes 1572868
  12.3 114.0 %all-to-all-start = ((bf16[256,64,128]{2,1,0:T(8,128)(2,1)}), bf16[256,64,128]{2,1,0:T(8,128)(2,1)}, u32[]{:S(2)}, u32[]{:S(2)}) async-start(bf16[256,64,128]{2,1,0:T(8,128)(2,1)} %bitcast.48), calls=%async_computation | async-start | bytes 8388608 | tf_op jit(solution)/shard_map/all_to_all | solution.py:352
  28.9 97.4 %copy-start.1 = (bf16[1,2048,512]{2,1,0:T(8,128)(2,1)S(1)}, bf16[1,2048,512]{2,1,0:T(8,128)(2,1)}, u32[]{:S(2)}) copy-start(bf16[1,2048,512]{2,1,0:T(8,128)(2,1)} %param.15) | copy-start | bytes 6291460
  28.9 84.4 %all-gather.3.cloned.1.call-start = ((), (), s32[]{:S(2)}) async-start(), calls=%async_computation.2 | async-start | bytes 5242880 | tf_op jit(solution)/shard_map/all_gather | solution.py:357
  138.7 8.6 %copy-start.10 = (bf16[2048]{0:T(1024)(128)(2,1)S(1)}, bf16[2048]{0:T(1024)(128)(2,1)}, u32[]{:S(2)}) copy-start(bf16[2048]{0:T(1024)(128)(2,1)} %param.21) | copy-start | bytes 12292
  138.7 8.6 %copy-start.3 = (bf16[128,2048]{1,0:T(8,128)(2,1)S(1)}, bf16[128,2048]{1,0:T(8,128)(2,1)}, u32[]{:S(2)}) copy-start(bf16[128,2048]{1,0:T(8,128)(2,1)} %cot_from.1) | copy-start | bytes 1572868
  138.7 8.8 %copy-start.4 = (bf16[128,2048]{1,0:T(8,128)(2,1)S(1)}, bf16[128,2048]{1,0:T(8,128)(2,1)}, u32[]{:S(2)}) copy-start(bf16[128,2048]{1,0:T(8,128)(2,1)} %tokens_from.1) | copy-start | bytes 1572868
  138.7 105.2 %all-to-all-start.1 = ((bf16[256,64,128]{2,1,0:T(8,128)(2,1)}), bf16[256,64,128]{2,1,0:T(8,128)(2,1)}, u32[]{:S(2)}, u32[]{:S(2)}) async-start(bf16[256,64,128]{2,1,0:T(8,128)(2,1)} %bitcast.50), calls=%async_computation.1 | async-start | bytes 8388608 | tf_op jit(solution)/shard_map/all_to_all | solution.py:352
  146.5 1.2 copy-start.9
  146.5 51.3 %all-gather.5.cloned.1.call-start = ((), (), s32[]{:S(2)}) async-start(), calls=%async_computation.3 | async-start | bytes 2621440 | tf_op jit(solution)/shard_map/all_gather | solution.py:362
  148.0 2.8 %copy-start.5 = (bf16[4096,512]{1,0:T(8,128)(2,1)S(1)}, bf16[4096,512]{1,0:T(8,128)(2,1)}, u32[]{:S(2)}) copy-start(bf16[4096,512]{1,0:T(8,128)(2,1)} %all-gather.3.cloned.1.call-done) | copy-start | bytes 12582916
  197.9 2.3 copy-start.2
  197.9 3.5 %copy-start.6 = (bf16[4096,512]{1,0:T(8,128)(2,1)S(1)}, bf16[4096,512]{1,0:T(8,128)(2,1)}, u32[]{:S(2)}) copy-start(bf16[4096,512]{1,0:T(8,128)(2,1)} %all-gather.3.cloned.1.call-done) | copy-start | bytes 12582916
  203.1 40.8 %copy-start = (f32[128,2]{0,1:T(2,128)S(1)}, f32[128,2]{0,1:T(2,128)}, u32[]{:S(2)}) copy-start(f32[128,2]{0,1:T(2,128)} %param.13) | copy-start | bytes 3076
Sparse Core Ops, SparseCore 0:
  31.6 81.7 all-gather.2
  149.2 48.6 all-gather.4

commit v6 on v5

--- a/solution.py
+++ b/solution.py
@@ -226,7 +226,8 @@
         pltpu.make_async_copy(rows_from.at[:, 0], outputs, came.at[0]),
         pltpu.make_async_copy(rows_from.at[:, 1], grads, came.at[1]),
     ]
-    copies[0].start()
+    for copy in copies:
+        copy.start()
     perm = swap_matrix()
     count = cot_ref.shape[0]
 
@@ -248,10 +249,9 @@
         return carry
 
     copies[0].wait()
-    copies[1].start()
-    lax.fori_loop(0, count, gather_output, 0, unroll=16)
+    lax.fori_loop(0, count, gather_output, 0, unroll=4)
     copies[1].wait()
-    lax.fori_loop(0, count, gather_grad, 0, unroll=16)
+    lax.fori_loop(0, count, gather_grad, 0, unroll=4)
     for group in range(count // TILE):
         at = slice(group * TILE, (group + 1) * TILE)
         both = jnp.concatenate(

time: 257 us -> 256 us (level)
  no operation moved by 1% of the time
where the time goes in v6:
time: 256 us
  waiting for transfers between devices  183 us (71%)
  starting transfers between devices  24.7 us (10%)
  Pallas kernels  22.3 us (9%)
  between operations  14.3 us (6%)
  matrix products  8.33 us (3%)
    all_gather x1, waiting for transfers between devices, local(): lax.all_gather(jnp.concatenate([shared_gate, shared_up], axis=0), 'tp', a...  83.2 us
    all_to_all x2, waiting for transfers between devices, exchange(): lax.all_to_all(rows.reshape(devices, -1, LANES), AXES, split_axis=0, conc...  53.4 us
    all_gather x1, waiting for transfers between devices, local(): all_down = lax.all_gather(shared_down, 'tp', axis=0, tiled=True)  46.3 us
    all_to_all x2, starting transfers between devices, exchange(): lax.all_to_all(rows.reshape(devices, -1, LANES), AXES, split_axis=0, conc...  24.5 us
    pallas_call x1, Pallas kernels, expert(): pl.pallas_call(expert_kernel, out_shape=jax.ShapeDtypeStruct(got.shape, j...  12.4 us
    dot_general x6, matrix products, dot(): return jnp.einsum(spec, a, b, preferred_element_type=jnp.float32)  8.09 us
  transfers between devices with their start and end apart: 4, of which 4 were waited for; matrix products, arithmetic and copies ran while one was open for 4% of the time, Pallas kernels for 0%

profile of v6, /device:TPU:1, one launch (start us, length us, event | category | flops | bytes accessed | tf_op | source)
XLA Modules:
  0.0 255.6 jit_solution(12833144048814535138)
XLA Ops:
  7.2 5.1 %shard_map.130 = bf16[256,2,2,16,128]{4,3,2,1,0:T(8,128)(2,1)} custom-call(s32[256]{0:T(256)} %bitcast.51, f32[256]{0:T(256)} %bitcast.45, bf16[128,2048]{1,0:T(8,128)(2,1)} %tokens_from.1, bf16[128,2048]{1,0:T(8,128)(2,1)} %cot_from.1), custom_call_target="tpu_custom_call" | custom-call | flops 268435456 | bytes 5242880 | tf_op jit(solution)/shard_map/pallas_call | solution.py:101
  12.2 0.0 copy-start.7
  12.3 16.7 %all-to-all-start = ((bf16[256,64,128]{2,1,0:T(8,128)(2,1)}), bf16[256,64,128]{2,1,0:T(8,128)(2,1)}, u32[]{:S(2)}, u32[]{:S(2)}) async-start(bf16[256,64,128]{2,1,0:T(8,128)(2,1)} %bitcast.48), calls=%async_computation | async-start | bytes 8388608 | tf_op jit(solution)/shard_map/all_to_all | solution.py:352
  28.9 0.0 copy-start.1
  28.9 0.0 all-gather.3.cloned.1.call-start
  29.0 1.1 pad_maximum_fusion
  30.1 0.0 all-gather.3.cloned.1.call-update
  30.1 83.2 %all-gather.3.cloned.1.call-done = bf16[4096,512]{1,0:T(8,128)(2,1)} async-done(((bf16[4096,128]{1,0:T(8,128)(2,1)}), bf16[4096,512]{1,0:T(8,128)(2,1)}) %all-gather.3.cloned.1.call-update) | async-done | bytes 4194320 | tf_op jit(solution)/shard_map/all_gather | solution.py:357
  113.3 13.0 %all-to-all-done = bf16[256,64,128]{2,1,0:T(8,128)(2,1)} async-done(((bf16[256,64,128]{2,1,0:T(8,128)(2,1)}), bf16[256,64,128]{2,1,0:T(8,128)(2,1)}, u32[]{:S(2)}, u32[]{:S(2)}) %all-to-all-start) | async-done | bytes 4194336 | tf_op jit(solution)/shard_map/all_to_all | solution.py:352
  126.3 12.4 %shard_map.131 = bf16[512,2,16,128]{3,2,1,0:T(8,128)(2,1)} custom-call(bf16[512,2,16,128]{3,2,1,0:T(8,128)(2,1)} %bitcast.5.got_from, bf16[2048,512]{1,0:T(8,128)(2,1)S(1)} %bitcast.47, bf16[2048,512]{1,0:T(8,128)(2,1)} %bitcast.54, bf16[512,2048]{1,0:T(8,128)(2,1)} %bitcast.55), custom_call_target="tpu_custom_call" | custom-call | flops 6442450944 | bytes 14680064 | tf_op jit(solution)/shard_map/pallas_call | solution.py:204
  138.7 0.0 copy-start.3
  138.7 0.0 copy-start.4
  138.7 7.8 %all-to-all-start.1 = ((bf16[256,64,128]{2,1,0:T(8,128)(2,1)}), bf16[256,64,128]{2,1,0:T(8,128)(2,1)}, u32[]{:S(2)}, u32[]{:S(2)}) async-start(bf16[256,64,128]{2,1,0:T(8,128)(2,1)} %bitcast.50), calls=%async_computation.1 | async-start | bytes 8388608 | tf_op jit(solution)/shard_map/all_to_all | solution.py:352
  146.5 0.2 all-gather.5.cloned.1.call-start
  146.8 0.5 all-gather.5.cloned.1.call-update
  147.3 0.1 copy.19
  147.5 0.2 fusion.20
  147.7 0.2 convert_reduce_fusion
  148.0 2.5 fusion.11
  150.5 0.3 copy-done.5
  150.8 0.7 fusion.14
  151.5 46.3 %all-gather.5.cloned.1.call-done = bf16[512,2048]{1,0:T(8,128)(2,1)} async-done(((bf16[128,2048]{1,0:T(8,128)(2,1)}), bf16[512,2048]{1,0:T(8,128)(2,1)}) %all-gather.5.cloned.1.call-update) | async-done | bytes 2097168 | tf_op jit(solution)/shard_map/all_gather | solution.py:362
  197.9 2.3 fusion.22
  200.2 0.8 fusion.23
  201.0 0.3 copy-done.6
  201.3 0.8 fusion.4
  202.2 0.9 fusion.8
  203.1 0.0 copy-start
  203.1 0.2 copy.21
  203.3 0.2 copy.20
  203.5 40.4 %all-to-all-done.1 = bf16[256,64,128]{2,1,0:T(8,128)(2,1)} async-done(((bf16[256,64,128]{2,1,0:T(8,128)(2,1)}), bf16[256,64,128]{2,1,0:T(8,128)(2,1)}, u32[]{:S(2)}, u32[]{:S(2)}) %all-to-all-start.1) | async-done | bytes 4194336 | tf_op jit(solution)/shard_map/all_to_all | solution.py:352
  243.9 4.8 %shard_map.132 = (bf16[128,2048]{1,0:T(8,128)(2,1)}, bf16[128,2048]{1,0:T(8,128)(2,1)}, f32[2,128]{1,0:T(2,128)}) custom-call(s32[256]{0:T(256)S(1)} %multiply_add_fusion.slot_ref, f32[256]{0:T(256)S(1)} %bitcast.46, bf16[512,2,16,128]{3,2,1,0:T(8,128)(2,1)} %bitcast.10.rows_from, bf16[128,16,128]{2,1,0:T(8,128)(2,1)S(1)} %bitcast.44, ...), custom_call_target="tpu_custom_call" | custom-call | flops 268435456 | bytes 8388608 | tf_op jit(solution)/shard_map/pallas_call | solution.py:278
  (20 shorter events, 0.1 us)
Async XLA Ops:
  12.2 16.8 %copy-start.7 = (bf16[2048,128]{1,0:T(8,128)(2,1)S(1)}, bf16[2048,128]{1,0:T(8,128)(2,1)}, u32[]{:S(2)}) copy-start(bf16[2048,128]{1,0:T(8,128)(2,1)} %param.19) | copy-start | bytes 1572868
  12.2 16.8 %copy-start.8 = (bf16[2048,128]{1,0:T(8,128)(2,1)S(1)}, bf16[2048,128]{1,0:T(8,128)(2,1)}, u32[]{:S(2)}) copy-start(bf16[2048,128]{1,0:T(8,128)(2,1)} %param.18) | copy-start | bytes 1572868
  12.3 114.0 %all-to-all-start = ((bf16[256,64,128]{2,1,0:T(8,128)(2,1)}), bf16[256,64,128]{2,1,0:T(8,128)(2,1)}, u32[]{:S(2)}, u32[]{:S(2)}) async-start(bf16[256,64,128]{2,1,0:T(8,128)(2,1)} %bitcast.48), calls=%async_computation | async-start | bytes 8388608 | tf_op jit(solution)/shard_map/all_to_all | solution.py:352
  28.9 97.4 %copy-start.1 = (bf16[1,2048,512]{2,1,0:T(8,128)(2,1)S(1)}, bf16[1,2048,512]{2,1,0:T(8,128)(2,1)}, u32[]{:S(2)}) copy-start(bf16[1,2048,512]{2,1,0:T(8,128)(2,1)} %param.15) | copy-start | bytes 6291460
  28.9 84.4 %all-gather.3.cloned.1.call-start = ((), (), s32[]{:S(2)}) async-start(), calls=%async_computation.2 | async-start | bytes 5242880 | tf_op jit(solution)/shard_map/all_gather | solution.py:357
  138.7 8.6 %copy-start.10 = (bf16[2048]{0:T(1024)(128)(2,1)S(1)}, bf16[2048]{0:T(1024)(128)(2,1)}, u32[]{:S(2)}) copy-start(bf16[2048]{0:T(1024)(128)(2,1)} %param.21) | copy-start | bytes 12292
  138.7 8.6 %copy-start.3 = (bf16[128,2048]{1,0:T(8,128)(2,1)S(1)}, bf16[128,2048]{1,0:T(8,128)(2,1)}, u32[]{:S(2)}) copy-start(bf16[128,2048]{1,0:T(8,128)(2,1)} %cot_from.1) | copy-start | bytes 1572868
  138.7 8.8 %copy-start.4 = (bf16[128,2048]{1,0:T(8,128)(2,1)S(1)}, bf16[128,2048]{1,0:T(8,128)(2,1)}, u32[]{:S(2)}) copy-start(bf16[128,2048]{1,0:T(8,128)(2,1)} %tokens_from.1) | copy-start | bytes 1572868
  138.7 105.2 %all-to-all-start.1 = ((bf16[256,64,128]{2,1,0:T(8,128)(2,1)}), bf16[256,64,128]{2,1,0:T(8,128)(2,1)}, u32[]{:S(2)}, u32[]{:S(2)}) async-start(bf16[256,64,128]{2,1,0:T(8,128)(2,1)} %bitcast.50), calls=%async_computation.1 | async-start | bytes 8388608 | tf_op jit(solution)/shard_map/all_to_all | solution.py:352
  146.5 1.2 copy-start.9
  146.5 51.3 %all-gather.5.cloned.1.call-start = ((), (), s32[]{:S(2)}) async-start(), calls=%async_computation.3 | async-start | bytes 2621440 | tf_op jit(solution)/shard_map/all_gather | solution.py:362
  148.0 2.8 %copy-start.5 = (bf16[4096,512]{1,0:T(8,128)(2,1)S(1)}, bf16[4096,512]{1,0:T(8,128)(2,1)}, u32[]{:S(2)}) copy-start(bf16[4096,512]{1,0:T(8,128)(2,1)} %all-gather.3.cloned.1.call-done) | copy-start | bytes 12582916
  197.9 2.3 copy-start.2
  197.9 3.5 %copy-start.6 = (bf16[4096,512]{1,0:T(8,128)(2,1)S(1)}, bf16[4096,512]{1,0:T(8,128)(2,1)}, u32[]{:S(2)}) copy-start(bf16[4096,512]{1,0:T(8,128)(2,1)} %all-gather.3.cloned.1.call-done) | copy-start | bytes 12582916
  203.1 40.8 %copy-start = (f32[128,2]{0,1:T(2,128)S(1)}, f32[128,2]{0,1:T(2,128)}, u32[]{:S(2)}) copy-start(f32[128,2]{0,1:T(2,128)} %param.13) | copy-start | bytes 3076
Sparse Core Ops, SparseCore 0:
  31.6 81.7 all-gather.2
  149.2 48.6 all-gather.4

commit v7 on v6

--- a/solution.py
+++ b/solution.py
@@ -220,38 +220,39 @@
 
 def combine_kernel(
     slot_ref, weight_ref, rows_from, cot_ref, shared_ref, shared_grad_ref, mixed_ref, grad_ref,
-    gate_ref, outputs, grads, mixed_tiles, grad_tiles, partial, came
+    gate_ref, tiles, mixed_tiles, grad_tiles, partial, came
 ):
+    size = tiles.shape[0] // PARTS
     copies = [
-        pltpu.make_async_copy(rows_from.at[:, 0], outputs, came.at[0]),
-        pltpu.make_async_copy(rows_from.at[:, 1], grads, came.at[1]),
+        pltpu.make_async_copy(
+            rows_from.at[pl.ds(part * size, size)],
+            tiles.at[pl.ds(part * size, size)],
+            came.at[part],
+        )
+        for part in range(PARTS)
     ]
     for copy in copies:
         copy.start()
     perm = swap_matrix()
     count = cot_ref.shape[0]
 
-    def gather_output(token, carry):
+    def gather(token, carry):
         cot = cot_ref[token].astype(jnp.float32)
         mixed = shared_ref[token]
+        grad = shared_grad_ref[token]
         for k in range(2):
-            output = outputs[slot_ref[k * count + token]].astype(jnp.float32)
+            at = slot_ref[k * count + token]
+            output = tiles[at, 0].astype(jnp.float32)
             mixed = mixed + weight_ref[k * count + token] * output
+            grad = grad + tiles[at, 1].astype(jnp.float32)
             partial[k, token] = jnp.sum((cot * output).reshape(2, 8, LANES), axis=0)
         mixed_tiles[token] = mixed.astype(jnp.bfloat16)
-        return carry
-
-    def gather_grad(token, carry):
-        grad = shared_grad_ref[token]
-        for k in range(2):
-            grad = grad + grads[slot_ref[k * count + token]].astype(jnp.float32)
         grad_tiles[token] = grad.astype(jnp.bfloat16)
         return carry
 
-    copies[0].wait()
-    lax.fori_loop(0, count, gather_output, 0, unroll=4)
-    copies[1].wait()
-    lax.fori_loop(0, count, gather_grad, 0, unroll=4)
+    for copy in copies:
+        copy.wait()
+    lax.fori_loop(0, count, gather, 0, unroll=4)
     for group in range(count // TILE):
         at = slice(group * TILE, (group + 1) * TILE)
         both = jnp.concatenate(
@@ -287,12 +288,11 @@
         + [pl.BlockSpec(memory_space=VMEM)] * 3,
         out_specs=[pl.BlockSpec(memory_space=VMEM)] * 3,
         scratch_shapes=[
-            pltpu.VMEM((rows.shape[0], TILE, LANES), jnp.bfloat16),
-            pltpu.VMEM((rows.shape[0], TILE, LANES), jnp.bfloat16),
+            pltpu.VMEM(rows.shape, jnp.bfloat16),
             pltpu.VMEM((count, TILE, LANES), jnp.bfloat16),
             pltpu.VMEM((count, TILE, LANES), jnp.bfloat16),
             pltpu.VMEM((2, count, 8, LANES), jnp.float32),
-            pltpu.SemaphoreType.DMA((2,)),
+            pltpu.SemaphoreType.DMA((PARTS,)),
         ],
         compiler_params=pltpu.CompilerParams(vmem_limit_bytes=32 << 20),
         cost_estimate=pl.CostEstimate(

time: 256 us -> 256 us (level)
  no operation moved by 1% of the time
where the time goes in v7:
time: 256 us
  waiting for transfers between devices  183 us (71%)
  starting transfers between devices  24.7 us (10%)
  Pallas kernels  22.5 us (9%)
  between operations  14.3 us (6%)
  matrix products  8.33 us (3%)
    all_gather x1, waiting for transfers between devices, local(): lax.all_gather(jnp.concatenate([shared_gate, shared_up], axis=0), 'tp', a...  83.2 us
    all_to_all x2, waiting for transfers between devices, exchange(): lax.all_to_all(rows.reshape(devices, -1, LANES), AXES, split_axis=0, conc...  53.4 us
    all_gather x1, waiting for transfers between devices, local(): all_down = lax.all_gather(shared_down, 'tp', axis=0, tiled=True)  46.3 us
    all_to_all x2, starting transfers between devices, exchange(): lax.all_to_all(rows.reshape(devices, -1, LANES), AXES, split_axis=0, conc...  24.5 us
    pallas_call x1, Pallas kernels, expert(): pl.pallas_call(expert_kernel, out_shape=jax.ShapeDtypeStruct(got.shape, j...  12.4 us
    dot_general x6, matrix products, dot(): return jnp.einsum(spec, a, b, preferred_element_type=jnp.float32)  8.09 us
  transfers between devices with their start and end apart: 4, of which 4 were waited for; matrix products, arithmetic and copies ran while one was open for 4% of the time, Pallas kernels for 0%

profile of v7, /device:TPU:1, one launch (start us, length us, event | category | flops | bytes accessed | tf_op | source)
XLA Modules:
  0.0 255.8 jit_solution(6253359543691779279)
XLA Ops:
  7.2 5.1 %shard_map.130 = bf16[256,2,2,16,128]{4,3,2,1,0:T(8,128)(2,1)} custom-call(s32[256]{0:T(256)} %bitcast.51, f32[256]{0:T(256)} %bitcast.45, bf16[128,2048]{1,0:T(8,128)(2,1)} %tokens_from.1, bf16[128,2048]{1,0:T(8,128)(2,1)} %cot_from.1), custom_call_target="tpu_custom_call" | custom-call | flops 268435456 | bytes 5242880 | tf_op jit(solution)/shard_map/pallas_call | solution.py:101
  12.2 0.0 copy-start.7
  12.3 16.7 %all-to-all-start = ((bf16[256,64,128]{2,1,0:T(8,128)(2,1)}), bf16[256,64,128]{2,1,0:T(8,128)(2,1)}, u32[]{:S(2)}, u32[]{:S(2)}) async-start(bf16[256,64,128]{2,1,0:T(8,128)(2,1)} %bitcast.48), calls=%async_computation | async-start | bytes 8388608 | tf_op jit(solution)/shard_map/all_to_all | solution.py:352
  28.9 0.0 copy-start.1
  28.9 0.0 all-gather.3.cloned.1.call-start
  29.0 1.1 pad_maximum_fusion
  30.1 0.0 all-gather.3.cloned.1.call-update
  30.1 83.2 %all-gather.3.cloned.1.call-done = bf16[4096,512]{1,0:T(8,128)(2,1)} async-done(((bf16[4096,128]{1,0:T(8,128)(2,1)}), bf16[4096,512]{1,0:T(8,128)(2,1)}) %all-gather.3.cloned.1.call-update) | async-done | bytes 4194320 | tf_op jit(solution)/shard_map/all_gather | solution.py:357
  113.3 13.0 %all-to-all-done = bf16[256,64,128]{2,1,0:T(8,128)(2,1)} async-done(((bf16[256,64,128]{2,1,0:T(8,128)(2,1)}), bf16[256,64,128]{2,1,0:T(8,128)(2,1)}, u32[]{:S(2)}, u32[]{:S(2)}) %all-to-all-start) | async-done | bytes 4194336 | tf_op jit(solution)/shard_map/all_to_all | solution.py:352
  126.3 12.4 %shard_map.131 = bf16[512,2,16,128]{3,2,1,0:T(8,128)(2,1)} custom-call(bf16[512,2,16,128]{3,2,1,0:T(8,128)(2,1)} %bitcast.5.got_from, bf16[2048,512]{1,0:T(8,128)(2,1)S(1)} %bitcast.47, bf16[2048,512]{1,0:T(8,128)(2,1)} %bitcast.54, bf16[512,2048]{1,0:T(8,128)(2,1)} %bitcast.55), custom_call_target="tpu_custom_call" | custom-call | flops 6442450944 | bytes 14680064 | tf_op jit(solution)/shard_map/pallas_call | solution.py:204
  138.7 0.0 copy-start.3
  138.7 0.0 copy-start.4
  138.7 7.8 %all-to-all-start.1 = ((bf16[256,64,128]{2,1,0:T(8,128)(2,1)}), bf16[256,64,128]{2,1,0:T(8,128)(2,1)}, u32[]{:S(2)}, u32[]{:S(2)}) async-start(bf16[256,64,128]{2,1,0:T(8,128)(2,1)} %bitcast.50), calls=%async_computation.1 | async-start | bytes 8388608 | tf_op jit(solution)/shard_map/all_to_all | solution.py:352
  146.5 0.2 all-gather.5.cloned.1.call-start
  146.8 0.5 all-gather.5.cloned.1.call-update
  147.3 0.1 copy.19
  147.5 0.2 fusion.20
  147.7 0.2 convert_reduce_fusion
  148.0 2.5 fusion.11
  150.5 0.3 copy-done.5
  150.8 0.7 fusion.14
  151.5 46.3 %all-gather.5.cloned.1.call-done = bf16[512,2048]{1,0:T(8,128)(2,1)} async-done(((bf16[128,2048]{1,0:T(8,128)(2,1)}), bf16[512,2048]{1,0:T(8,128)(2,1)}) %all-gather.5.cloned.1.call-update) | async-done | bytes 2097168 | tf_op jit(solution)/shard_map/all_gather | solution.py:362
  197.9 2.3 fusion.22
  200.2 0.8 fusion.23
  201.0 0.3 copy-done.6
  201.3 0.8 fusion.4
  202.2 0.9 fusion.8
  203.1 0.0 copy-start
  203.1 0.2 copy.21
  203.3 0.2 copy.20
  203.5 40.4 %all-to-all-done.1 = bf16[256,64,128]{2,1,0:T(8,128)(2,1)} async-done(((bf16[256,64,128]{2,1,0:T(8,128)(2,1)}), bf16[256,64,128]{2,1,0:T(8,128)(2,1)}, u32[]{:S(2)}, u32[]{:S(2)}) %all-to-all-start.1) | async-done | bytes 4194336 | tf_op jit(solution)/shard_map/all_to_all | solution.py:352
  243.9 5.1 %shard_map.132 = (bf16[128,2048]{1,0:T(8,128)(2,1)}, bf16[128,2048]{1,0:T(8,128)(2,1)}, f32[2,128]{1,0:T(2,128)}) custom-call(s32[256]{0:T(256)S(1)} %multiply_add_fusion.slot_ref, f32[256]{0:T(256)S(1)} %bitcast.46, bf16[512,2,16,128]{3,2,1,0:T(8,128)(2,1)} %bitcast.10.rows_from, bf16[128,16,128]{2,1,0:T(8,128)(2,1)S(1)} %bitcast.44, ...), custom_call_target="tpu_custom_call" | custom-call | flops 268435456 | bytes 8388608 | tf_op jit(solution)/shard_map/pallas_call | solution.py:279
  (20 shorter events, 0.1 us)
Async XLA Ops:
  12.2 16.8 %copy-start.7 = (bf16[2048,128]{1,0:T(8,128)(2,1)S(1)}, bf16[2048,128]{1,0:T(8,128)(2,1)}, u32[]{:S(2)}) copy-start(bf16[2048,128]{1,0:T(8,128)(2,1)} %param.19) | copy-start | bytes 1572868
  12.2 16.8 %copy-start.8 = (bf16[2048,128]{1,0:T(8,128)(2,1)S(1)}, bf16[2048,128]{1,0:T(8,128)(2,1)}, u32[]{:S(2)}) copy-start(bf16[2048,128]{1,0:T(8,128)(2,1)} %param.18) | copy-start | bytes 1572868
  12.3 114.0 %all-to-all-start = ((bf16[256,64,128]{2,1,0:T(8,128)(2,1)}), bf16[256,64,128]{2,1,0:T(8,128)(2,1)}, u32[]{:S(2)}, u32[]{:S(2)}) async-start(bf16[256,64,128]{2,1,0:T(8,128)(2,1)} %bitcast.48), calls=%async_computation | async-start | bytes 8388608 | tf_op jit(solution)/shard_map/all_to_all | solution.py:352
  28.9 97.4 %copy-start.1 = (bf16[1,2048,512]{2,1,0:T(8,128)(2,1)S(1)}, bf16[1,2048,512]{2,1,0:T(8,128)(2,1)}, u32[]{:S(2)}) copy-start(bf16[1,2048,512]{2,1,0:T(8,128)(2,1)} %param.15) | copy-start | bytes 6291460
  28.9 84.4 %all-gather.3.cloned.1.call-start = ((), (), s32[]{:S(2)}) async-start(), calls=%async_computation.2 | async-start | bytes 5242880 | tf_op jit(solution)/shard_map/all_gather | solution.py:357
  138.7 8.6 %copy-start.10 = (bf16[2048]{0:T(1024)(128)(2,1)S(1)}, bf16[2048]{0:T(1024)(128)(2,1)}, u32[]{:S(2)}) copy-start(bf16[2048]{0:T(1024)(128)(2,1)} %param.21) | copy-start | bytes 12292
  138.7 8.6 %copy-start.3 = (bf16[128,2048]{1,0:T(8,128)(2,1)S(1)}, bf16[128,2048]{1,0:T(8,128)(2,1)}, u32[]{:S(2)}) copy-start(bf16[128,2048]{1,0:T(8,128)(2,1)} %cot_from.1) | copy-start | bytes 1572868
  138.7 8.8 %copy-start.4 = (bf16[128,2048]{1,0:T(8,128)(2,1)S(1)}, bf16[128,2048]{1,0:T(8,128)(2,1)}, u32[]{:S(2)}) copy-start(bf16[128,2048]{1,0:T(8,128)(2,1)} %tokens_from.1) | copy-start | bytes 1572868
  138.7 105.2 %all-to-all-start.1 = ((bf16[256,64,128]{2,1,0:T(8,128)(2,1)}), bf16[256,64,128]{2,1,0:T(8,128)(2,1)}, u32[]{:S(2)}, u32[]{:S(2)}) async-start(bf16[256,64,128]{2,1,0:T(8,128)(2,1)} %bitcast.50), calls=%async_computation.1 | async-start | bytes 8388608 | tf_op jit(solution)/shard_map/all_to_all | solution.py:352
  146.5 1.2 copy-start.9
  146.5 51.3 %all-gather.5.cloned.1.call-start = ((), (), s32[]{:S(2)}) async-start(), calls=%async_computation.3 | async-start | bytes 2621440 | tf_op jit(solution)/shard_map/all_gather | solution.py:362
  148.0 2.8 %copy-start.5 = (bf16[4096,512]{1,0:T(8,128)(2,1)S(1)}, bf16[4096,512]{1,0:T(8,128)(2,1)}, u32[]{:S(2)}) copy-start(bf16[4096,512]{1,0:T(8,128)(2,1)} %all-gather.3.cloned.1.call-done) | copy-start | bytes 12582916
  197.9 2.3 copy-start.2
  197.9 3.5 %copy-start.6 = (bf16[4096,512]{1,0:T(8,128)(2,1)S(1)}, bf16[4096,512]{1,0:T(8,128)(2,1)}, u32[]{:S(2)}) copy-start(bf16[4096,512]{1,0:T(8,128)(2,1)} %all-gather.3.cloned.1.call-done) | copy-start | bytes 12582916
  203.1 40.8 %copy-start = (f32[128,2]{0,1:T(2,128)S(1)}, f32[128,2]{0,1:T(2,128)}, u32[]{:S(2)}) copy-start(f32[128,2]{0,1:T(2,128)} %param.13) | copy-start | bytes 3076
Sparse Core Ops, SparseCore 0:
  31.6 81.7 all-gather.2
  149.2 48.6 all-gather.4
